TPU v7x, 32 devices: a whole 2x2x4 slice. The times are simulated.
32 devices in a mesh: tm: 8 (over z, y), table: 4 (over x, core).
Axes of the slice: x: 2, y: 2, z: 4, core: 2. Of those that a mesh axis runs over, the one named last changes fastest.
Arguments:
- out_grad: bfloat16 [4, 16384, 512], P('table', 'tm'), may hold values from -1.1953125 to 1.1953125
- bc_proj: bfloat16 [4, 16384, 128], P('table', 'tm'), may hold values from -0.18847656 to 0.18847656
- decay_log: float32 [4, 8, 16384], P('table', None, 'tm'), may hold values from -1 to 0
- skip_gain: float32 [8], replicated, may hold values from 0.5 to 1.5
- owner: int32 [4, 16384, 1], P('table', 'tm'), may hold values from 0 to 31; in each aligned block of 2048 rows (0 to 2047, 2048 to 4095, ..., all dimensions but the last counted through in order) at most 128 rows name the same one
- item_row: int32 [4, 16384], P('table', 'tm'), may hold values from 0 to 1535
- table: bfloat16 [49152, 512], P(('tm', 'table')), may hold values from -3 to 3
- accum: float32 [49152, 512], P(('tm', 'table')), may hold values from 1 to 10
Outputs:
- new_table: bfloat16 [49152, 512], P(('tm', 'table'))
- new_accum: float32 [49152, 512], P(('tm', 'table'))
Inputs may be any that keep to these rules, and one draw needn't show every extreme that they name: Among the events of one device at most 128 have the same owner; in every draw some device has exactly 128 events for some owner.
All inputs are finite; a program needn't handle non-finite values.
Results may differ from a plain program's by a relative error of at most 0.0018.
Values may be sent and summed in bfloat16 or wider, within the bound.
No kernel may reach another device: no remote copies, remote signals or barrier semaphores. Data moves between devices by JAX's collectives and lax.ppermute only.
A program may use at most 128 MiB of HBM per device.

v0:
```python
import jax
import jax.numpy as jnp
from jax import lax
from jax.sharding import PartitionSpec as P

HEADS = 8
STATE = 64
GROUP = 256


learn_rate = 1.0


def entering(x, axis, combine, identity):
    size, mine = (lax.axis_size(axis), lax.axis_index(axis))
    everything = jax.tree.map(lambda part: lax.all_gather(part, axis), x)
    start = jax.tree.map(
        lambda part, zero: jnp.broadcast_to(jnp.asarray(zero, part.dtype), part.shape), x, identity
    )

    def hop(k, before):
        at = size - 1 - k
        reached = at > mine
        new = combine(before, jax.tree.map(lambda part: part[at], everything))
        return jax.tree.map(lambda a, b: jnp.where(reached, a, b), new, before)

    return lax.fori_loop(0, size, hop, start)


def block_end(grad_block, c_block, decay_block):
    cumul = jnp.cumsum(decay_block, axis=1)
    length = grad_block.shape[0]
    scaled = (
        grad_block.astype(jnp.float32).reshape(length, HEADS, -1) * jnp.exp(cumul).T[:, :, None]
    )
    ends = jnp.einsum(
        "thp,tn->hpn", scaled, c_block.astype(jnp.float32), precision=lax.Precision.HIGHEST
    )
    return (cumul[:, -1], ends)


def fold_back(carry, item):
    log_end, end_term = item
    return (end_term + jnp.exp(log_end)[..., None, None] * carry, carry)


def block_rows(grad_block, b_block, c_block, decay_block, carried, skip_gain):
    length = grad_block.shape[0]
    cumul = jnp.cumsum(decay_block, axis=1)
    scores = jnp.dot(c_block, b_block.T, preferred_element_type=jnp.float32)
    later = jnp.arange(length)[:, None] >= jnp.arange(length)[None, :]
    gaps = jnp.where(later[None], cumul[:, :, None] - cumul[:, None, :], 0.0)
    mixing = jnp.where(later[None], jnp.exp(gaps) * scores[None], 0.0).astype(jnp.bfloat16)
    heads_grad = grad_block.reshape(length, HEADS, -1)
    inner = jnp.einsum("hts,thp->shp", mixing, heads_grad, preferred_element_type=jnp.float32)
    fading = jnp.exp(cumul[:, -1:] - cumul)
    carried_part = (
        jnp.einsum(
            "hpn,sn->shp", carried, b_block.astype(jnp.float32), precision=lax.Precision.HIGHEST
        )
        * fading.T[:, :, None]
    )
    total = inner + carried_part + skip_gain[None, :, None] * heads_grad.astype(jnp.float32)
    return total.reshape(length, -1).astype(jnp.bfloat16)


def compose(earlier, later):
    return (earlier[0] + later[0], later[1] + jnp.exp(later[0])[..., None] * earlier[1])


def on_device(out_grad, bc_proj, decay_log, skip_gain, owner, item_row, table, accum):
    users, events, width = out_grad.shape
    blocks = events // GROUP
    head_dim = width // HEADS
    grad_blocks = out_grad.reshape(users * blocks, GROUP, width)
    b_blocks = bc_proj[:, :, :STATE].reshape(users * blocks, GROUP, STATE)
    c_blocks = bc_proj[:, :, STATE:].reshape(users * blocks, GROUP, STATE)
    decay_blocks = (
        decay_log.reshape(users, HEADS, blocks, GROUP)
        .transpose(0, 2, 1, 3)
        .reshape(users * blocks, HEADS, GROUP)
    )
    log_ends, end_terms = jax.vmap(block_end)(grad_blocks, c_blocks, decay_blocks)
    log_seq = log_ends.reshape(users, blocks, HEADS).transpose(1, 0, 2)
    end_seq = end_terms.reshape(users, blocks, HEADS, head_dim, STATE).transpose(1, 0, 2, 3, 4)
    empty = jnp.zeros((users, HEADS, head_dim, STATE), jnp.float32)
    device_end, _ = lax.scan(fold_back, empty, (log_seq, end_seq), reverse=True)
    device_log = jnp.sum(log_seq, axis=0)
    device_flat = device_end.reshape(users, HEADS, head_dim * STATE)
    identity = (
        jnp.zeros((users, HEADS), jnp.float32),
        jnp.zeros((users, HEADS, head_dim * STATE), jnp.float32),
    )
    _, incoming_flat = entering((device_log, device_flat), "tm", compose, identity)
    incoming = incoming_flat.reshape(users, HEADS, head_dim, STATE)
    _, carried_seq = lax.scan(fold_back, incoming, (log_seq, end_seq), reverse=True)
    carried = carried_seq.transpose(1, 0, 2, 3, 4).reshape(users * blocks, HEADS, head_dim, STATE)
    rows = jax.vmap(lambda a, b, c, d, e: block_rows(a, b, c, d, e, skip_gain))(
        grad_blocks, b_blocks, c_blocks, decay_blocks, carried
    )
    flat_rows = rows.reshape(users * events, width)
    target = owner.reshape(-1)
    local_row = item_row.reshape(-1)
    tm_count = lax.axis_size("tm")
    table_count = lax.axis_size("table")
    holders = tm_count * table_count
    capacity = max(2, 2 * users * events // holders)
    hits = (target[:, None] == jnp.arange(holders, dtype=jnp.int32)[None, :]).astype(jnp.int32)
    before = jnp.cumsum(hits, axis=0) - hits
    slot = jnp.sum(before * hits, axis=1)
    position = target * capacity + slot
    send_rows = jnp.zeros((holders * capacity, width), jnp.bfloat16).at[position].set(flat_rows)
    send_ids = jnp.zeros((holders * capacity,), jnp.int32).at[position].set(local_row)
    send_rows = send_rows.reshape(tm_count, table_count, capacity, width)
    send_ids = send_ids.reshape(tm_count, table_count, capacity)
    got_rows, got_ids = (
        lax.all_to_all(
            lax.all_to_all(send_rows, "tm", split_axis=0, concat_axis=0, tiled=True),
            "table",
            split_axis=1,
            concat_axis=1,
            tiled=True,
        ),
        lax.all_to_all(
            lax.all_to_all(send_ids, "tm", split_axis=0, concat_axis=0, tiled=True),
            "table",
            split_axis=1,
            concat_axis=1,
            tiled=True,
        ),
    )
    owned = table.shape[0]
    summed = jax.ops.segment_sum(
        got_rows.reshape(-1, width).astype(jnp.float32), got_ids.reshape(-1), num_segments=owned
    )
    new_accum = accum + summed * summed
    new_table = (table.astype(jnp.float32) - learn_rate * summed / jnp.sqrt(new_accum)).astype(
        jnp.bfloat16
    )
    return (new_table, new_accum)


def solution(mesh):
    placed = (
        P("table", "tm", None),
        P("table", "tm", None),
        P("table", None, "tm"),
        P(),
        P("table", "tm", None),
        P("table", "tm"),
        P(("tm", "table"), None),
        P(("tm", "table"), None),
    )
    return jax.shard_map(
        on_device,
        mesh=mesh,
        in_specs=placed,
        out_specs=(P(("tm", "table"), None), P(("tm", "table"), None)),
        check_vma=False,
    )
```

profile of v0, /device:TPU:0, one launch (start us, length us, event | category | flops | bytes accessed | tf_op | source)
XLA Modules:
  0.0 347.6 jit_solution(2246600932414258855)
XLA Ops:
  7.2 8.1 %reduce-window.16 = f32[8,8,2,128]{3,1,2,0:T(8,128)S(1)} reduce-window(f32[8,8,2,128]{3,1,2,0:T(8,128)} %bitcast.131, f32[]{:T(128)} %constant.139.clone.1), window={size=1x1x1x128 pad=0_0x0_0x0_0x127_0}, to_apply=%region_4.5 | reduce-window | flops 2080768 | bytes 131076 | tf_op jit(solution)/shard_map/reduce-window.2
  17.1 1.4 fusion.31
  18.5 3.7 %reshape.223 = bf16[8,256,8,64]{3,2,1,0:T(8,128)(2,1)} reshape(bf16[1,2048,512]{2,1,0:T(8,128)(2,1)S(1)} %copy-done.1) | data formatting | bytes 4194304 | tf_op jit(solution)/shard_map/vmap()/reshape;reshape | solution.py:54
  22.2 5.1 %copy.114 = bf16[8,256,8,64]{1,3,2,0:T(8,128)(2,1)} copy(bf16[8,256,8,64]{3,2,1,0:T(8,128)(2,1)} %reshape.223) | data formatting | bytes 4194304 | tf_op jit(solution)/shard_map/vmap()/reshape;reshape | solution.py:54
  27.3 3.8 %fusion.20 = f32[8,1,8,64,64]{4,3,2,1,0:T(8,128)S(1)} fusion(bf16[8,256,64,1]{2,1,3,0:T(8,128)(2,1)S(1)} %bitcast.122, bf16[8,256,8,64]{1,3,2,0:T(8,128)(2,1)} %copy.114, f32[8,256,8]{1,2,0:T(8,128)S(1)} %get-tuple-element.473), kind=kOutput, calls=%fused_computation.37 | convolution fusion | flops 807403520 | bytes 3473408 | tf_op jit(solution)/shard_map/vmap(thp,tn->hpn)/dot_general | solution.py:36
  31.1 1.1 while.48
  33.7 15.9 %reduce-window.14 = s32[32,16,128]{2,1,0:T(8,128)S(1)} reduce-window(s32[32,16,128]{2,1,0:T(8,128)} %fusion.25, s32[]{:T(128)} %copy.169), window={size=1x1x128 pad=0_0x0_0x127_0}, to_apply=%region_0.0 | reduce-window | flops 8323072 | bytes 524292 | tf_op jit(solution)/shard_map/reduce-window
  50.4 1.2 copy.129
  52.1 8.8 %scatter_custom_fusion = s32[4096]{0:T(1024)} fusion(s32[2048]{0:T(1024)S(1)} %bitcast.136, s32[2048]{0:T(1024)} %bitcast.139, s32[]{:T(128)} %copy.169), kind=kCustom, calls=%fused_computation.57 | custom fusion | bytes 16896 | tf_op jit(solution)/shard_map/scatter | solution.py:113
  60.9 7.3 %all-to-all-start = ((s32[8,4,128]{2,1,0:T(4,128)}), s32[8,4,128]{2,1,0:T(4,128)S(1)}, u32[]{:S(2)}, u32[]{:S(2)}) async-start(s32[8,4,128]{2,1,0:T(4,128)} %bitcast.12), calls=%async_computation | async-start | bytes 32768 | tf_op jit(solution)/shard_map/all_to_all | solution.py:125
  68.2 1.2 dynamic-slice
  70.9 22.0 %all-reduce = f32[64]{0:T(128)S(1)} all-reduce(f32[64]{0:T(128)S(1)} %dynamic-update-slice), channel_id=2, replica_groups=mesh['tm'=8,'table'=4] {'tm'}, use_global_device_ids=true, to_apply=%add | all-reduce | flops 64 | bytes 512
  93.6 1.5 exponential_bitcast_fusion.2
  95.2 1.8 fusion.32
  97.0 8.3 %while.49 = (s32[]{:T(128)}, f32[1,8,4096]{2,1,0:T(8,128)S(1)}, s32[]{:T(128)}, f32[8,1,8,4096]{3,2,1,0:T(8,128)}, f32[8,1,8]{2,1,0:T(1,128)S(1)}, /*index=5*/s32[]{:T(128)}, s32[]{:T(128)}, s32[]{:T(128)}, s32[]{:T(128)}) while((s32[]{:T(128)}, f32[1,8,4096]{2,1,0:T(8,128)S(1)}, s32[]{:T(128)}, f32[8,1,8,4096]{3,2,1,0:T(8,128)}, ...), condition=%wide.region_10.11_spmd.clone, body=%wide.region_9.10_spmd.clone.sunk | while | flops 131080 | bytes 393479 | solution.py:27
  99.0 1.0 fusion.41
  105.4 1.6 broadcast_in_dim.71
  106.9 12.1 %while.47 = (s32[]{:T(128)}, f32[1,8,64,64]{3,2,1,0:T(8,128)S(1)}, f32[8,1,8,64,64]{4,3,2,1,0:T(8,128)}, f32[8,1,8,64,64]{4,3,2,1,0:T(8,128)S(1)}, f32[8,1,8]{2,1,0:T(1,128)}, /*index=5*/s32[]{:T(128)}, s32[]{:T(128)}) while((s32[]{:T(128)}, f32[1,8,64,64]{3,2,1,0:T(8,128)S(1)}, f32[8,1,8,64,64]{4,3,2,1,0:T(8,128)}, ...), condition=%wide.region_12.13_spmd, body=%wide.region_11.12_spmd.sunk | while | flops 65539 | bytes 786629 | solution.py:96
  119.1 3.6 %fusion.15 = f32[8,8,64,256]{3,2,1,0:T(8,128)S(1)} fusion(bf16[8,256,64,1]{2,1,3,0:T(8,128)(2,1)S(1)} %bitcast.125, f32[8,1,8,64,64]{4,3,2,1,0:T(8,128)} %get-tuple-element.323), kind=kOutput, calls=%fused_computation.32 | convolution fusion | flops 805306368 | bytes 5505024 | tf_op jit(solution)/shard_map/vmap(hpn,sn->shp)/dot_general | solution.py:58
  122.8 5.3 %fusion.13 = bf16[8,256,8,64]{1,3,2,0:T(8,128)(2,1)S(1)} fusion(bf16[8,256,8,64]{1,3,2,0:T(8,128)(2,1)S(1)} %copy-done, f32[8,8,64,256]{3,2,1,0:T(8,128)S(1)} %fusion.15, f32[8,256,256]{2,1,0:T(8,128)S(1)} %copy-done.2, f32[8,8,256]{2,1,0:T(8,128)S(1)} %copy-done.4, pred[256,256]{1,0:T(8,128)(4,1)S(1)} %copy-done.6, f32[8]{0:T(128)S(1)} %copy-done.10, ...), kind=kOutput, calls=%fused_computation.27 | convolution fusion | flops 564133888 | bytes 10682400 | tf_op jit(solution)/shard_map/vmap(hts,thp->shp)/dot_general | solution.py:55
  128.1 3.6 %copy.140 = bf16[8,256,8,64]{3,2,1,0:T(8,128)(2,1)} copy(bf16[8,256,8,64]{1,3,2,0:T(8,128)(2,1)S(1)} %fusion.13) | data formatting | bytes 4194304 | tf_op jit(solution)/shard_map/vmap()/convert_element_type | solution.py:64
  131.7 5.4 %reshape.222 = bf16[2048,512]{1,0:T(8,128)(2,1)S(1)} reshape(bf16[8,256,8,64]{3,2,1,0:T(8,128)(2,1)} %copy.140) | data formatting | bytes 4194304 | tf_op jit(solution)/shard_map/vmap()/convert_element_type | solution.py:64
  137.1 12.3 %scatter_custom_fusion.1 = bf16[4096,512]{1,0:T(8,128)(2,1)} fusion(s32[2048]{0:T(1024)} %bitcast.137, bf16[2048,512]{1,0:T(8,128)(2,1)S(1)} %reshape.222, bf16[]{:T(256)} %constant.143.clone.1), kind=kCustom, calls=%fused_computation.35 | custom fusion | bytes 4194816 | tf_op jit(solution)/shard_map/scatter | solution.py:112
  149.4 4.5 %all-to-all-start.2 = ((bf16[8,4,128,512]{3,2,1,0:T(8,128)(2,1)}), bf16[8,4,128,512]{3,2,1,0:T(8,128)(2,1)}, u32[]{:S(2)}, u32[]{:S(2)}) async-start(bf16[8,4,128,512]{3,2,1,0:T(8,128)(2,1)} %bitcast.120), calls=%async_computation.2 | async-start | bytes 8388608 | tf_op jit(solution)/shard_map/all_to_all | solution.py:118
  154.5 88.5 %all-to-all-done.2 = bf16[8,4,128,512]{3,2,1,0:T(8,128)(2,1)} async-done(((bf16[8,4,128,512]{3,2,1,0:T(8,128)(2,1)}), bf16[8,4,128,512]{3,2,1,0:T(8,128)(2,1)}, u32[]{:S(2)}, u32[]{:S(2)}) %all-to-all-start.2) | async-done | bytes 4194336 | tf_op jit(solution)/shard_map/all_to_all | solution.py:118
  243.1 3.3 all-to-all-start.1
  246.3 4.6 %copy.125 = bf16[8,4,128,512]{3,2,0,1:T(8,128)(2,1)} copy(bf16[8,4,128,512]{3,2,1,0:T(8,128)(2,1)} %all-to-all-done.2) | data formatting | bytes 8388608 | tf_op jit(solution)/shard_map/all_to_all | solution.py:118
  250.9 5.1 %all-to-all-start.3 = ((bf16[8,4,128,512]{3,2,0,1:T(8,128)(2,1)}), bf16[8,4,128,512]{3,2,0,1:T(8,128)(2,1)}, u32[]{:S(2)}, u32[]{:S(2)}) async-start(bf16[8,4,128,512]{3,2,0,1:T(8,128)(2,1)} %copy.125), calls=%async_computation.3 | async-start | bytes 8388608 | tf_op jit(solution)/shard_map/all_to_all | solution.py:117
  256.0 48.2 %all-to-all-done.3 = bf16[8,4,128,512]{3,2,0,1:T(8,128)(2,1)} async-done(((bf16[8,4,128,512]{3,2,0,1:T(8,128)(2,1)}), bf16[8,4,128,512]{3,2,0,1:T(8,128)(2,1)}, u32[]{:S(2)}, u32[]{:S(2)}) %all-to-all-start.3) | async-done | bytes 4194336 | tf_op jit(solution)/shard_map/all_to_all | solution.py:117
  304.2 4.6 %copy.126 = bf16[8,4,128,512]{3,2,1,0:T(8,128)(2,1)} copy(bf16[8,4,128,512]{3,2,0,1:T(8,128)(2,1)} %all-to-all-done.3) | data formatting | bytes 8388608 | tf_op jit(solution)/shard_map/all_to_all | solution.py:117
  308.8 26.4 %scatter_custom_fusion.2 = f32[1536,512]{1,0:T(8,128)S(1)} fusion(s32[4096]{0:T(1024)S(1)} %bitcast.135, bf16[4096,512]{1,0:T(8,128)(2,1)} %bitcast.121, f32[]{:T(128)} %constant.139.clone.1), kind=kCustom, calls=%fused_computation.16 | custom fusion | flops 4194304 | bytes 7340036 | tf_op jit(solution)/shard_map/scatter-add | solution.py:133
  335.2 5.5 %subtract_convert_fusion = (bf16[1536,512]{1,0:T(8,128)(2,1)}, f32[1536,512]{1,0:T(8,128)}) fusion(f32[1536,512]{1,0:T(8,128)S(1)} %scatter_custom_fusion.2, bf16[1536,512]{1,0:T(8,128)(2,1)} %param.20, f32[1536,512]{1,0:T(8,128)} %param.21), kind=kLoop, calls=%fused_computation.30 | loop fusion | flops 4718592 | bytes 12582912 | tf_op jit(solution)/shard_map/convert_element_type | solution.py:137
  (105 shorter events, 26.6 us)
Async XLA Ops:
  7.2 11.4 %copy-start.1 = (bf16[1,2048,512]{2,1,0:T(8,128)(2,1)S(1)}, bf16[1,2048,512]{2,1,0:T(8,128)(2,1)}, u32[]{:S(2)}) copy-start(bf16[1,2048,512]{2,1,0:T(8,128)(2,1)} %param.14) | copy-start | bytes 6291460
  7.2 89.8 %all-gather.3.cloned.1.call-start = ((), (), s32[]{:S(2)}) async-start(), calls=%async_computation.4 | async-start | bytes 1179648 | tf_op jit(solution)/shard_map/all_gather | solution.py:16
  15.8 0.6 copy-start.3
  31.1 1.9 copy-start.5
  32.2 19.5 %copy-start.8 = (f32[8,1,8]{2,1,0:T(1,128)}, f32[8,1,8]{2,1,0:T(1,128)S(1)}, u32[]{:S(2)}) copy-start(f32[8,1,8]{2,1,0:T(1,128)S(1)} %get-tuple-element.644) | copy-start | bytes 772
  52.1 16.1 %copy-start.9 = (s32[2048,1]{0,1:T(1,128)}, s32[2048,1]{0,1:T(1,128)S(1)}, u32[]{:S(2)}) copy-start(s32[2048,1]{0,1:T(1,128)S(1)} %compare_select_fusion) | copy-start | bytes 24580
  60.9 88.5 %all-to-all-start = ((s32[8,4,128]{2,1,0:T(4,128)}), s32[8,4,128]{2,1,0:T(4,128)S(1)}, u32[]{:S(2)}, u32[]{:S(2)}) async-start(s32[8,4,128]{2,1,0:T(4,128)} %bitcast.12), calls=%async_computation | async-start | bytes 32768 | tf_op jit(solution)/shard_map/all_to_all | solution.py:125
  119.0 3.7 %copy-start = (bf16[8,256,8,64]{1,3,2,0:T(8,128)(2,1)S(1)}, bf16[8,256,8,64]{1,3,2,0:T(8,128)(2,1)}, u32[]{:S(2)}) copy-start(bf16[8,256,8,64]{1,3,2,0:T(8,128)(2,1)} %copy.114) | copy-start | bytes 6291460
  119.0 3.7 %copy-start.2 = (f32[8,256,256]{2,1,0:T(8,128)S(1)}, f32[8,256,256]{2,1,0:T(8,128)}, u32[]{:S(2)}) copy-start(f32[8,256,256]{2,1,0:T(8,128)} %fusion.32) | copy-start | bytes 6291460
  119.1 3.7 %copy-start.4 = (f32[8,8,256]{2,1,0:T(8,128)S(1)}, f32[8,8,256]{2,1,0:T(8,128)}, u32[]{:S(2)}) copy-start(f32[8,8,256]{2,1,0:T(8,128)} %copy-done.3) | copy-start | bytes 196612
  119.1 3.7 %copy-start.6 = (pred[256,256]{1,0:T(8,128)(4,1)S(1)}, pred[256,256]{1,0:T(8,128)(4,1)}, u32[]{:S(2)}) copy-start(pred[256,256]{1,0:T(8,128)(4,1)} %iota_compare_fusion) | copy-start | bytes 196612
  119.1 3.7 %copy-start.7 = (f32[8,256,8]{1,2,0:T(8,128)S(1)}, f32[8,256,8]{1,2,0:T(8,128)}, u32[]{:S(2)}) copy-start(f32[8,256,8]{1,2,0:T(8,128)} %exponential_bitcast_fusion.2) | copy-start | bytes 196612
  119.1 3.7 %copy-start.10 = (f32[8]{0:T(128)S(1)}, f32[8]{0:T(128)}, u32[]{:S(2)}) copy-start(f32[8]{0:T(128)} %param.17) | copy-start | bytes 100
  149.4 93.7 %all-to-all-start.2 = ((bf16[8,4,128,512]{3,2,1,0:T(8,128)(2,1)}), bf16[8,4,128,512]{3,2,1,0:T(8,128)(2,1)}, u32[]{:S(2)}, u32[]{:S(2)}) async-start(bf16[8,4,128,512]{3,2,1,0:T(8,128)(2,1)} %bitcast.120), calls=%async_computation.2 | async-start | bytes 8388608 | tf_op jit(solution)/shard_map/all_to_all | solution.py:118
  243.1 7.9 %all-to-all-start.1 = ((s32[8,4,128]{2,0,1:T(8,128)}), s32[8,4,128]{2,0,1:T(8,128)S(1)}, u32[]{:S(2)}, u32[]{:S(2)}) async-start(s32[8,4,128]{2,0,1:T(8,128)} %copy.105), calls=%async_computation.1 | async-start | bytes 32768 | tf_op jit(solution)/shard_map/all_to_all | solution.py:124
  250.9 53.3 %all-to-all-start.3 = ((bf16[8,4,128,512]{3,2,0,1:T(8,128)(2,1)}), bf16[8,4,128,512]{3,2,0,1:T(8,128)(2,1)}, u32[]{:S(2)}, u32[]{:S(2)}) async-start(bf16[8,4,128,512]{3,2,0,1:T(8,128)(2,1)} %copy.125), calls=%async_computation.3 | async-start | bytes 8388608 | tf_op jit(solution)/shard_map/all_to_all | solution.py:117
Sparse Core Ops, SparseCore 0:
  33.1 43.1 all-gather.2
where the time goes:
time: 351 us; the launch traced here: 348 us
  waiting for transfers between devices  137 us (39%)
  other arithmetic  69.7 us (20%)
  local copies, waits for them, and re-layouts  68.7 us (20%)
  blocking collectives  22 us (6%)
  starting transfers between devices  20.2 us (6%)
  between operations  15 us (4%)
  matrix products  14.5 us (4%)
    all_to_all x1, waiting for transfers between devices, on_device(): lax.all_to_all(send_rows, 'tm', split_axis=0, concat_axis=0, tiled=True)  88.5 us
    all_to_all x1, waiting for transfers between devices, on_device(): lax.all_to_all(lax.all_to_all(send_rows, 'tm', split_axis=0, concat_axis=...  48.2 us
    scatter-add x1, other arithmetic, on_device(): jax.ops.segment_sum(got_rows.reshape(-1, width).astype(jnp.float32), got_...  26.4 us
    another operation x5, other arithmetic  24.4 us
    unnamed x1, blocking collectives  22 us
    scatter x1, local copies, waits for them, and re-layouts, on_device(): jnp.zeros((holders * capacity, width), jnp.bfloat16).at[position]  12.3 us
    convert_element_type x2, local copies, waits for them, and re-layouts, block_rows(): return total.reshape(length, -1).astype(jnp.bfloat16)  9.03 us
    scatter x1, local copies, waits for them, and re-layouts, on_device(): jnp.zeros((holders * capacity,), jnp.int32).at[position].set(local_row)  8.78 us
  transfers between devices with their start and end apart: 5, of which 2 were waited for; matrix products, arithmetic and copies ran while one was open for 26% of the time, Pallas kernels for 0%

commit v1 on v0

v1 whole, which is shorter than its diff:
```python
import functools

import jax
import jax.numpy as jnp
from jax import lax
from jax.experimental import pallas as pl
from jax.experimental.pallas import tpu as pltpu
from jax.sharding import PartitionSpec as P

HEADS = 8
STATE = 64
GROUP = 256
BOTH = ("tm", "table")
VMEM_BYTES = 48 * 1024 * 1024

learn_rate = 1.0

f32 = jnp.float32
bf16 = jnp.bfloat16
HIGHEST = lax.Precision.HIGHEST


def params():
    return pltpu.CompilerParams(vmem_limit_bytes=VMEM_BYTES)


def cost(flops, moved, exps=0):
    return pl.CostEstimate(flops=flops, bytes_accessed=moved, transcendentals=exps)


def spread(columns, width):
    rows = columns.shape[0]
    head_dim = width // HEADS
    low = lax.broadcasted_iota(jnp.int32, (rows, 2 * head_dim), 1) < head_dim
    parts = [
        jnp.where(low, columns[:, h : h + 1], columns[:, h + 1 : h + 2]) for h in range(0, HEADS, 2)
    ]
    return jnp.concatenate(parts, axis=1)


def cumul_columns(decay):
    shape = (GROUP, GROUP)
    upto = (lax.broadcasted_iota(jnp.int32, shape, 1) <= lax.broadcasted_iota(jnp.int32, shape, 0))
    return lax.dot_general(
        jnp.where(upto, 1.0, 0.0), decay, (((1,), (1,)), ((), ())), precision=HIGHEST,
        preferred_element_type=f32,
    )


def cumul_rows(decay):
    shape = (GROUP, GROUP)
    upto = (lax.broadcasted_iota(jnp.int32, shape, 0) <= lax.broadcasted_iota(jnp.int32, shape, 1))
    return jnp.dot(
        decay, jnp.where(upto, 1.0, 0.0), precision=HIGHEST, preferred_element_type=f32
    )


def two_parts(x):
    high = x.astype(bf16)
    return high, (x - high.astype(f32)).astype(bf16)


def state_kernel(grad_ref, bc_ref, decay_ref, carried_ref, after_ref, end_ref, log_ref, state, log):
    width = grad_ref.shape[1]

    @pl.when(pl.program_id(0) == 0)
    def _():
        state[...] = jnp.zeros_like(state)
        log[...] = jnp.zeros_like(log)

    cumul = cumul_columns(decay_ref[...])
    scaled = grad_ref[...].astype(f32) * spread(jnp.exp(cumul), width)
    c = bc_ref[:, STATE:]
    high, low = two_parts(scaled)
    dims = (((0,), (0,)), ((), ()))
    ends = lax.dot_general(c, high, dims, preferred_element_type=f32) + lax.dot_general(
        c, low, dims, preferred_element_type=f32
    )
    carried_ref[0] = state[...]
    after_ref[0] = log[...]
    log_end = spread(cumul[GROUP - 1 :, :], width)
    state[...] = ends + jnp.exp(log_end) * state[...]
    log[...] = log[...] + log_end
    end_ref[...] = state[...]
    log_ref[...] = log[...]


def state_of(grad, bc, decay):
    events, width = grad.shape
    blocks = events // GROUP
    back = lambda i: (blocks - 1 - i, 0)
    return pl.pallas_call(
        state_kernel,
        grid=(blocks,),
        in_specs=[
            pl.BlockSpec((GROUP, width), back),
            pl.BlockSpec((GROUP, 2 * STATE), back),
            pl.BlockSpec((HEADS, GROUP), lambda i: (0, blocks - 1 - i)),
        ],
        out_specs=[
            pl.BlockSpec((1, STATE, width), lambda i: (blocks - 1 - i, 0, 0)),
            pl.BlockSpec((1, 1, width), lambda i: (blocks - 1 - i, 0, 0)),
            pl.BlockSpec((STATE, width), lambda i: (0, 0)),
            pl.BlockSpec((1, width), lambda i: (0, 0)),
        ],
        out_shape=[
            jax.ShapeDtypeStruct((blocks, STATE, width), f32),
            jax.ShapeDtypeStruct((blocks, 1, width), f32),
            jax.ShapeDtypeStruct((STATE, width), f32),
            jax.ShapeDtypeStruct((1, width), f32),
        ],
        scratch_shapes=[pltpu.VMEM((STATE, width), f32), pltpu.VMEM((1, width), f32)],
        compiler_params=params(),
        cost_estimate=cost(4 * events * width * STATE, 4 * events * width),
        name="state",
    )(grad, bc, decay)


def local_kernel(grad_ref, bc_ref, decay_ref, skip_ref, carried_ref, after_ref, out_ref, fade_ref):
    width = grad_ref.shape[1]
    head_dim = width // HEADS
    decay = decay_ref[...]
    columns, rows = cumul_columns(decay), cumul_rows(decay)
    b, c = bc_ref[:, :STATE], bc_ref[:, STATE:]
    scores = lax.dot_general(b, c, (((1,), (1,)), ((), ())), preferred_element_type=f32)
    shape = (GROUP, GROUP)
    later = lax.broadcasted_iota(jnp.int32, shape, 1) >= lax.broadcasted_iota(jnp.int32, shape, 0)
    scores = jnp.where(later, scores, 0.0)
    grad = grad_ref[...]
    inner = []
    for h in range(HEADS):
        gaps = jnp.where(later, rows[h : h + 1, :] - columns[:, h : h + 1], 0.0)
        mixing = (jnp.exp(gaps) * scores).astype(bf16)
        inner.append(
            jnp.dot(
                mixing, grad[:, h * head_dim : (h + 1) * head_dim], preferred_element_type=f32
            )
        )
    fading = spread(jnp.exp(columns[GROUP - 1 :, :] - columns), width)
    high, low = two_parts(carried_ref[0])
    carried = jnp.dot(b, high, preferred_element_type=f32) + jnp.dot(
        b, low, preferred_element_type=f32
    )
    gain = spread(skip_ref[...], width)
    out_ref[...] = jnp.concatenate(inner, axis=1) + carried * fading + gain * grad.astype(f32)
    fade_ref[...] = fading * jnp.exp(after_ref[0])


def local_rows(grad, bc, decay, skip, carried, after):
    events, width = grad.shape
    blocks = events // GROUP
    at = lambda i: (i, 0)
    return pl.pallas_call(
        local_kernel,
        grid=(blocks,),
        in_specs=[
            pl.BlockSpec((GROUP, width), at),
            pl.BlockSpec((GROUP, 2 * STATE), at),
            pl.BlockSpec((HEADS, GROUP), lambda i: (0, i)),
            pl.BlockSpec((1, HEADS), lambda i: (0, 0)),
            pl.BlockSpec((1, STATE, width), lambda i: (i, 0, 0)),
            pl.BlockSpec((1, 1, width), lambda i: (i, 0, 0)),
        ],
        out_specs=[pl.BlockSpec((GROUP, width), at), pl.BlockSpec((GROUP, width), at)],
        out_shape=[jax.ShapeDtypeStruct((events, width), f32)] * 2,
        compiler_params=params(),
        cost_estimate=cost(
            blocks * GROUP * GROUP * (2 * width + 8 * HEADS), 10 * events * width,
            blocks * GROUP * GROUP * HEADS,
        ),
        name="local",
    )(grad, bc, decay, skip, carried, after)


def slots_kernel(capacity, owner_ref, row_ref, place_ref, ids_ref):
    holders = ids_ref.shape[0]
    shape = (GROUP, GROUP)
    before = lax.broadcasted_iota(jnp.int32, shape, 0) < lax.broadcasted_iota(jnp.int32, shape, 1)
    before = jnp.where(before, 1.0, 0.0).astype(bf16)
    count = jnp.zeros((holders, 1), f32)
    names = lax.broadcasted_iota(jnp.int32, (holders, GROUP), 0)
    ranks = lax.broadcasted_iota(jnp.int32, (capacity, GROUP), 0)
    high = jnp.zeros((holders, capacity), f32)
    low = jnp.zeros((holders, capacity), f32)
    across = (((1,), (1,)), ((), ()))
    for k in range(owner_ref.shape[0]):
        target = owner_ref[k : k + 1, :]
        hit = names == target
        hits = jnp.where(hit, 1.0, 0.0)
        earlier = jnp.dot(hits.astype(bf16), before, preferred_element_type=f32) + count
        rank = jnp.sum(hits * earlier, axis=0, keepdims=True).astype(jnp.int32)
        count = count + jnp.sum(hits, axis=1, keepdims=True)
        place_ref[k : k + 1, :] = target * capacity + rank
        ranked = jnp.where(ranks == rank, 1.0, 0.0).astype(bf16)
        named = row_ref[k : k + 1, :] + 1
        upper = (hits * (named // 64).astype(f32)).astype(bf16)
        lower = (hits * (named % 64).astype(f32)).astype(bf16)
        high = high + lax.dot_general(upper, ranked, across, preferred_element_type=f32)
        low = low + lax.dot_general(lower, ranked, across, preferred_element_type=f32)
    ids_ref[...] = (high * 64.0 + low).astype(jnp.int32)


def slots(owner, row, holders, capacity):
    return pl.pallas_call(
        functools.partial(slots_kernel, capacity),
        out_shape=[
            jax.ShapeDtypeStruct(owner.shape, jnp.int32),
            jax.ShapeDtypeStruct((holders, capacity), jnp.int32),
        ],
        compiler_params=params(),
        cost_estimate=cost(2 * holders * owner.size * (GROUP + 2 * capacity), 8 * owner.size),
        name="slots",
    )(owner, row)


def send_kernel(tile, place_ref, bc_ref, local_ref, fade_ref, state_ref, out_ref, rows):
    step = pl.program_id(0)

    @pl.when(step == 0)
    def _():
        high, low = two_parts(state_ref[...])
        for k in range(place_ref.shape[0]):
            at = pl.ds(k * GROUP, GROUP)
            b = bc_ref[at, :STATE]
            part = jnp.dot(b, high, preferred_element_type=f32) + jnp.dot(
                b, low, preferred_element_type=f32
            )
            rows[at, :] = (local_ref[at, :] + part * fade_ref[at, :]).astype(bf16)

    places = lax.broadcasted_iota(jnp.int32, (tile, GROUP), 0) + step * tile
    total = jnp.zeros(out_ref.shape, f32)
    for k in range(place_ref.shape[0]):
        chosen = jnp.where(places == place_ref[k : k + 1, :], 1.0, 0.0).astype(bf16)
        total = total + jnp.dot(
            chosen, rows[pl.ds(k * GROUP, GROUP), :], preferred_element_type=f32
        )
    out_ref[...] = total.astype(bf16)


def sent_rows(place, bc, local, fade, state, places):
    events, width = local.shape
    tile = 512
    whole = lambda a: pl.BlockSpec(a.shape, lambda i: (0,) * a.ndim)
    return pl.pallas_call(
        functools.partial(send_kernel, tile),
        grid=(places // tile,),
        in_specs=[whole(place), whole(bc), whole(local), whole(fade), whole(state)],
        out_specs=pl.BlockSpec((tile, width), lambda i: (i, 0)),
        out_shape=jax.ShapeDtypeStruct((places, width), bf16),
        scratch_shapes=[pltpu.VMEM((events, width), bf16)],
        compiler_params=params(),
        cost_estimate=cost(2 * places * events * width, 12 * events * width),
        name="send",
    )(place, bc, local, fade, state)


def update_kernel(tile, ids_ref, got_ref, table_ref, accum_ref, new_table_ref, new_accum_ref):
    names = lax.broadcasted_iota(jnp.int32, (tile, GROUP), 0) + (pl.program_id(0) * tile + 1)
    total = jnp.zeros(accum_ref.shape, f32)
    for k in range(ids_ref.shape[0]):
        chosen = jnp.where(names == ids_ref[k : k + 1, :], 1.0, 0.0).astype(bf16)
        total = total + jnp.dot(
            chosen, got_ref[pl.ds(k * GROUP, GROUP), :], preferred_element_type=f32
        )
    accum = accum_ref[...] + total * total
    new_accum_ref[...] = accum
    new_table_ref[...] = (
        table_ref[...].astype(f32) - learn_rate * total / jnp.sqrt(accum)
    ).astype(bf16)


def updated(ids, got, table, accum):
    owned, width = table.shape
    tile = 512
    at = lambda i: (i, 0)
    return pl.pallas_call(
        functools.partial(update_kernel, tile),
        grid=(owned // tile,),
        in_specs=[
            pl.BlockSpec(ids.shape, lambda i: (0, 0)),
            pl.BlockSpec(got.shape, lambda i: (0, 0)),
            pl.BlockSpec((tile, width), at),
            pl.BlockSpec((tile, width), at),
        ],
        out_specs=[pl.BlockSpec((tile, width), at)] * 2,
        out_shape=[
            jax.ShapeDtypeStruct(table.shape, bf16),
            jax.ShapeDtypeStruct(accum.shape, f32),
        ],
        compiler_params=params(),
        cost_estimate=cost(2 * owned * got.shape[0] * width, 12 * owned * width),
        name="update",
    )(ids, got, table, accum)


def entering(end, log):
    size = lax.axis_size("tm")
    rows, width = end.shape
    parts = jnp.concatenate(
        [
            end.reshape(size, rows // size, width),
            jnp.broadcast_to(log[None], (size, 1, width)),
        ],
        axis=1,
    )
    parts = lax.all_to_all(parts, "tm", split_axis=0, concat_axis=0, tiled=True)
    ends, fades = parts[:, :-1], jnp.exp(parts[:, -1:])
    state = jnp.zeros((rows // size, width), f32)
    into = [state]
    for k in range(size - 1, 0, -1):
        state = ends[k] + fades[k] * state
        into.append(state)
    into = jnp.stack(into[::-1])
    into = lax.all_to_all(into, "tm", split_axis=0, concat_axis=0, tiled=True)
    return into.reshape(rows, width)


def on_device(out_grad, bc_proj, decay_log, skip_gain, owner, item_row, table, accum):
    users, events, width = out_grad.shape
    grad = out_grad.reshape(events, width)
    bc = bc_proj.reshape(events, 2 * STATE)
    decay = decay_log.reshape(HEADS, events)
    holders = lax.axis_size("tm") * lax.axis_size("table")
    capacity = 2 * events // holders

    carried, after, end, log = state_of(grad, bc, decay)
    place, ids = slots(
        owner.reshape(events // GROUP, GROUP), item_row.reshape(events // GROUP, GROUP),
        holders, capacity,
    )
    state = entering(end, log)
    got_ids = lax.all_to_all(ids, BOTH, split_axis=0, concat_axis=0, tiled=True)
    local, fade = local_rows(grad, bc, decay, skip_gain.reshape(1, HEADS), carried, after)
    rows = sent_rows(place, bc, local, fade, state, holders * capacity)
    got = lax.all_to_all(
        rows.reshape(holders, capacity, width), BOTH, split_axis=0, concat_axis=0, tiled=True
    ).reshape(holders * capacity, width)
    return updated(got_ids.reshape(-1, GROUP), got, table, accum)


def solution(mesh):
    placed = (
        P("table", "tm", None),
        P("table", "tm", None),
        P("table", None, "tm"),
        P(),
        P("table", "tm", None),
        P("table", "tm"),
        P(("tm", "table"), None),
        P(("tm", "table"), None),
    )
    return jax.shard_map(
        on_device,
        mesh=mesh,
        in_specs=placed,
        out_specs=(P(("tm", "table"), None), P(("tm", "table"), None)),
        check_vma=False,
    )
```

time: 351 us -> 191 us (0.54)
  other arithmetic: 69.7 us -> 5.03 us
  local copies, waits for them, and re-layouts: 68.7 us -> 11.4 us
  Pallas kernels: 0 us -> 48.5 us
  waiting for transfers between devices: 137 us -> 93.2 us
  matrix products: 14.5 us -> 0 us
  between operations: 15 us -> 0.81 us
  blocking collectives: 22 us -> 16 us
  starting transfers between devices: 20.2 us -> 15.5 us
    pallas_call x0 -> x5, Pallas kernels: none -> 48.5 us  [the longest x1 14.8 us: sent_rows(): pl.pallas_call(functools.partial(send_kernel, tile), grid=(places // tile...]
    all_to_all x4 -> x3, waiting for transfers between devices: 137 us -> 93.2 us  [the longest x1 93.2 us: on_device(): lax.all_to_all(rows.reshape(holders, capacity, width), BOTH, split_axis=0...]
    scatter-add x1 -> x0, other arithmetic: 26.4 us -> none  [on_device(): jax.ops.segment_sum(got_rows.reshape(-1, width).astype(jnp.float32), got_...]
    another operation x5 -> x0, other arithmetic: 24.4 us -> none
    unnamed x1 -> x0, blocking collectives: 22 us -> none
    scatter x2 -> x0, local copies, waits for them, and re-layouts: 21 us -> none  [the longest x1 12.3 us: on_device(): jnp.zeros((holders * capacity, width), jnp.bfloat16).at[position]]
    all_to_all x0 -> x1, blocking collectives: none -> 16 us  [entering(): parts = lax.all_to_all(parts, 'tm', split_axis=0, concat_axis=0, tiled=True)]
    dot_general x4 -> x0, matrix products: 14.5 us -> none  [the longest x1 5.27 us: block_rows(): jnp.einsum('hts,thp->shp', mixing, heads_grad, preferred_element_type=jnp...]
  transfers between devices with their start and end apart: 5 -> 3, of which waited for: 2 -> 1; matrix products, arithmetic and copies ran while one was open for 26% -> 1% of each run, Pallas kernels for 0% -> 7%
where the time goes in v1:
time: 191 us; the launch traced here: 190 us
  waiting for transfers between devices  93.2 us (49%)
  Pallas kernels  48.5 us (25%)
  blocking collectives  16 us (8%)
  starting transfers between devices  15.5 us (8%)
  local copies, waits for them, and re-layouts  11.4 us (6%)
  other arithmetic  5.03 us (3%)
    all_to_all x1, waiting for transfers between devices, on_device(): lax.all_to_all(rows.reshape(holders, capacity, width), BOTH, split_axis=0...  93.2 us
    all_to_all x1, blocking collectives, entering(): parts = lax.all_to_all(parts, 'tm', split_axis=0, concat_axis=0, tiled=True)  16 us
    pallas_call x1, Pallas kernels, sent_rows(): pl.pallas_call(functools.partial(send_kernel, tile), grid=(places // tile...  14.8 us
    pallas_call x1, Pallas kernels, local_rows(): pl.pallas_call(local_kernel, grid=(blocks,), in_specs=[pl.BlockSpec((GROU...  11.9 us
    pallas_call x1, Pallas kernels, updated(): pl.pallas_call(functools.partial(update_kernel, tile), grid=(owned // til...  11.3 us
    unnamed x31, local copies, waits for them, and re-layouts  10.8 us
    pallas_call x1, Pallas kernels, state_of(): pl.pallas_call(state_kernel, grid=(blocks,), in_specs=[pl.BlockSpec((GROU...  8.31 us
    all_to_all x1, starting transfers between devices, on_device(): got_ids = lax.all_to_all(ids, BOTH, split_axis=0, concat_axis=0, tiled=True)  5.99 us
  transfers between devices with their start and end apart: 3, of which 1 were waited for; matrix products, arithmetic and copies ran while one was open for 1% of the time, Pallas kernels for 7%

profile of v1, /device:TPU:0, one launch (start us, length us, event | category | flops | bytes accessed | tf_op | source)
XLA Modules:
  0.0 190.5 jit_solution(5628910715559394414)
XLA Ops:
  0.7 1.6 copy-done.1
  2.2 1.0 copy-done.3
  3.3 0.8 copy-done.5
  4.1 8.3 %state.1 = (f32[8,64,512]{2,1,0:T(8,128)S(1)}, f32[8,1,512]{2,1,0:T(1,128)S(1)}, f32[64,512]{1,0:T(8,128)S(1)}, f32[1,512]{1,0:T(1,128)S(1)}) custom-call(bf16[2048,512]{1,0:T(8,128)(2,1)S(1)} %bitcast.21, bf16[2048,128]{1,0:T(8,128)(2,1)S(1)} %bitcast.23, f32[8,2048]{1,0:T(8,128)S(1)} %bitcast.28), custom_call_target="tpu_custom_call" | custom-call | flops 268435456 | bytes 4194304 | tf_op jit(solution)/shard_map/state/pallas_call | solution.py:92
  12.5 0.0 copy-start.9
  12.5 1.0 copy-done.9
  13.5 16.0 %all_to_all.24 = f32[8,9,512]{2,1,0:T(8,128)S(1)} all-to-all(f32[8,9,512]{2,1,0:T(8,128)S(1)} %pad_maximum_fusion), channel_id=1, replica_groups=mesh['tm'=8,'table'=4] {'tm'}, dimensions={0} | all-to-all | bytes 294912 | tf_op jit(solution)/shard_map/all_to_all | solution.py:306
  29.5 0.6 constant_dynamic-update-slice_fusion.7
  30.1 0.6 constant_dynamic-update-slice_fusion.6
  30.8 0.6 constant_dynamic-update-slice_fusion.5
  31.4 0.6 constant_dynamic-update-slice_fusion.4
  32.0 0.6 constant_dynamic-update-slice_fusion.3
  32.6 0.6 constant_dynamic-update-slice_fusion.2
  33.2 0.6 constant_dynamic-update-slice_fusion.1
  33.8 0.6 constant_dynamic-update-slice_fusion
  34.4 3.6 %all-to-all-start.2 = ((f32[8,8,512]{2,1,0:T(8,128)}), f32[8,8,512]{2,1,0:T(8,128)S(1)}, u32[]{:S(2)}, u32[]{:S(2)}) async-start(f32[8,8,512]{2,1,0:T(8,128)} %constant_dynamic-update-slice_fusion), calls=%async_computation.2 | async-start | bytes 262144 | tf_op jit(solution)/shard_map/all_to_all | solution.py:314
  38.0 0.5 broadcast.133
  38.5 0.6 reduce.9
  39.2 0.6 reduce.10
  39.8 2.2 %slots.1 = (s32[8,256]{1,0:T(8,128)S(1)}, s32[32,128]{1,0:T(8,128)}) custom-call(s32[8,256]{1,0:T(8,128)S(1)} %reshape.213.owner_ref, s32[8,256]{1,0:T(8,128)S(1)} %reshape.214.row_ref), custom_call_target="tpu_custom_call" | custom-call | flops 67108864 | bytes 16384 | tf_op jit(solution)/shard_map/slots/pallas_call | solution.py:204
  42.0 0.0 copy-start.10
  42.0 1.2 copy-done.10
  43.3 11.9 %local.1 = (f32[2048,512]{1,0:T(8,128)}, f32[2048,512]{1,0:T(8,128)}) custom-call(bf16[2048,512]{1,0:T(8,128)(2,1)S(1)} %bitcast.22, bf16[2048,128]{1,0:T(8,128)(2,1)S(1)} %bitcast.24, f32[8,2048]{1,0:T(8,128)S(1)} %bitcast.29, f32[1,8]{1,0:T(1,128)S(1)} %bitcast.31, f32[8,64,512]{2,1,0:T(8,128)S(1)} %copy-done.10, f32[8,1,512]{2,1,0:T(1,128)S(1)} %get-tuple-element.13.after_ref), custom_call_target="tpu_custom_call" | custom-call | flops 570425344 | bytes 10485760 | tf_op jit(solution)/shard_map/local/pallas_call | solution.py:153
  55.1 6.0 %all-to-all-start = ((s32[32,1,128]{2,1,0:T(1,128)}), s32[32,1,128]{2,1,0:T(1,128)S(1)}, u32[]{:S(2)}, u32[]{:S(2)}) async-start(s32[32,1,128]{2,1,0:T(1,128)} %bitcast.1), calls=%async_computation | async-start | bytes 32768 | tf_op jit(solution)/shard_map/all_to_all | solution.py:332
  61.1 14.8 %send.1 = bf16[4096,512]{1,0:T(8,128)(2,1)S(1)} custom-call(s32[8,256]{1,0:T(8,128)S(1)} %get-tuple-element.11.place_ref, bf16[2048,128]{1,0:T(8,128)(2,1)S(1)} %bitcast.25, f32[2048,512]{1,0:T(8,128)} %get-tuple-element.14.local_ref, f32[2048,512]{1,0:T(8,128)} %get-tuple-element.15.fade_ref, f32[64,512]{1,0:T(8,128)S(1)} %bitcast.27), custom_call_target="tpu_custom_call" | custom-call | flops 8589934592 | bytes 12582912 | tf_op jit(solution)/shard_map/send/pallas_call | solution.py:244
  75.9 2.0 %copy-done = bf16[4096,512]{1,0:T(8,128)(2,1)} copy-done((bf16[4096,512]{1,0:T(8,128)(2,1)}, bf16[4096,512]{1,0:T(8,128)(2,1)S(1)}, u32[]{:S(2)}) %copy-start) | copy-done | bytes 4194328
  77.9 0.0 all-to-all-done
  77.9 6.0 %all-to-all-start.3 = ((bf16[32,128,512]{2,1,0:T(8,128)(2,1)}), bf16[32,128,512]{2,1,0:T(8,128)(2,1)}, u32[]{:S(2)}, u32[]{:S(2)}) async-start(bf16[32,128,512]{2,1,0:T(8,128)(2,1)} %bitcast.20), calls=%async_computation.3 | async-start | bytes 8388608 | tf_op jit(solution)/shard_map/all_to_all | solution.py:335
  83.9 0.7 reduce.11
  84.6 93.2 %all-to-all-done.3 = bf16[32,128,512]{2,1,0:T(8,128)(2,1)} async-done(((bf16[32,128,512]{2,1,0:T(8,128)(2,1)}), bf16[32,128,512]{2,1,0:T(8,128)(2,1)}, u32[]{:S(2)}, u32[]{:S(2)}) %all-to-all-start.3) | async-done | bytes 4194336 | tf_op jit(solution)/shard_map/all_to_all | solution.py:335
  177.8 1.4 copy-done.8
  179.2 11.3 %update.1 = (bf16[1536,512]{1,0:T(8,128)(2,1)}, f32[1536,512]{1,0:T(8,128)}) custom-call(s32[16,256]{1,0:T(8,128)S(1)} %reshape.215.ids_ref, bf16[4096,512]{1,0:T(8,128)(2,1)} %bitcast.17.got_ref, bf16[1536,512]{1,0:T(8,128)(2,1)S(1)} %copy-done.8, f32[1536,512]{1,0:T(8,128)S(1)} %copy-done.7), custom_call_target="tpu_custom_call" | custom-call | flops 6442450944 | bytes 9437184 | tf_op jit(solution)/shard_map/update/pallas_call | solution.py:276
  (27 shorter events, 0.1 us)
Async XLA Ops:
  0.6 41.4 %copy-start.11 = (f32[8]{0:T(128)S(1)}, f32[8]{0:T(128)}, u32[]{:S(2)}) copy-start(f32[8]{0:T(128)} %param.11) | copy-start | bytes 100
  0.6 1.6 copy-start.1
  2.2 1.0 copy-start.3
  3.3 0.8 copy-start.5
  4.1 34.4 %copy-start.12 = (s32[1,2048,1]{1,2,0:T(1,128)S(1)}, s32[1,2048,1]{1,2,0:T(1,128)}, u32[]{:S(2)}) copy-start(s32[1,2048,1]{1,2,0:T(1,128)} %param.12) | copy-start | bytes 24580
  4.1 35.1 %copy-start.13 = (s32[1,2048]{1,0:T(1,128)S(1)}, s32[1,2048]{1,0:T(1,128)}, u32[]{:S(2)}) copy-start(s32[1,2048]{1,0:T(1,128)} %param.13) | copy-start | bytes 24580
  4.1 37.9 %copy-start.2 = (bf16[1,2048,512]{2,1,0:T(8,128)(2,1)S(1)}, bf16[1,2048,512]{2,1,0:T(8,128)(2,1)}, u32[]{:S(2)}) copy-start(bf16[1,2048,512]{2,1,0:T(8,128)(2,1)} %param.8) | copy-start | bytes 6291460
  4.1 37.9 %copy-start.4 = (bf16[1,2048,128]{2,1,0:T(8,128)(2,1)S(1)}, bf16[1,2048,128]{2,1,0:T(8,128)(2,1)}, u32[]{:S(2)}) copy-start(bf16[1,2048,128]{2,1,0:T(8,128)(2,1)} %param.9) | copy-start | bytes 1572868
  4.1 37.9 %copy-start.6 = (f32[1,8,2048]{2,1,0:T(8,128)S(1)}, f32[1,8,2048]{2,1,0:T(8,128)}, u32[]{:S(2)}) copy-start(f32[1,8,2048]{2,1,0:T(8,128)} %param.10) | copy-start | bytes 196612
  12.5 1.0 copy-start.9
  34.4 20.7 %all-to-all-start.2 = ((f32[8,8,512]{2,1,0:T(8,128)}), f32[8,8,512]{2,1,0:T(8,128)S(1)}, u32[]{:S(2)}, u32[]{:S(2)}) async-start(f32[8,8,512]{2,1,0:T(8,128)} %constant_dynamic-update-slice_fusion), calls=%async_computation.2 | async-start | bytes 262144 | tf_op jit(solution)/shard_map/all_to_all | solution.py:314
  42.0 1.2 copy-start.10
  55.1 22.8 %all-to-all-start = ((s32[32,1,128]{2,1,0:T(1,128)}), s32[32,1,128]{2,1,0:T(1,128)S(1)}, u32[]{:S(2)}, u32[]{:S(2)}) async-start(s32[32,1,128]{2,1,0:T(1,128)} %bitcast.1), calls=%async_computation | async-start | bytes 32768 | tf_op jit(solution)/shard_map/all_to_all | solution.py:332
  75.9 2.0 %copy-start = (bf16[4096,512]{1,0:T(8,128)(2,1)}, bf16[4096,512]{1,0:T(8,128)(2,1)S(1)}, u32[]{:S(2)}) copy-start(bf16[4096,512]{1,0:T(8,128)(2,1)S(1)} %send.1) | copy-start | bytes 12582916
  77.9 99.8 %copy-start.7 = (f32[1536,512]{1,0:T(8,128)S(1)}, f32[1536,512]{1,0:T(8,128)}, u32[]{:S(2)}) copy-start(f32[1536,512]{1,0:T(8,128)} %accum_ref.1) | copy-start | bytes 9437188
  77.9 99.8 %all-to-all-start.3 = ((bf16[32,128,512]{2,1,0:T(8,128)(2,1)}), bf16[32,128,512]{2,1,0:T(8,128)(2,1)}, u32[]{:S(2)}, u32[]{:S(2)}) async-start(bf16[32,128,512]{2,1,0:T(8,128)(2,1)} %bitcast.20), calls=%async_computation.3 | async-start | bytes 8388608 | tf_op jit(solution)/shard_map/all_to_all | solution.py:335
  177.8 1.4 copy-start.8

commit v2 on v1

v2 whole, which is shorter than its diff:
```python
import functools

import jax
import jax.numpy as jnp
from jax import lax
from jax.experimental import pallas as pl
from jax.experimental.pallas import tpu as pltpu
from jax.sharding import PartitionSpec as P

HEADS = 8
STATE = 64
GROUP = 256
ALIGN = 16
BOTH = ("tm", "table")
VMEM_BYTES = 60 * 1024 * 1024

learn_rate = 1.0

f32 = jnp.float32
bf16 = jnp.bfloat16


def params():
    return pltpu.CompilerParams(vmem_limit_bytes=VMEM_BYTES)


def cost(flops, moved, exps=0):
    return pl.CostEstimate(flops=flops, bytes_accessed=moved, transcendentals=exps)


def spread(columns, width):
    rows = columns.shape[0]
    head_dim = width // HEADS
    low = lax.broadcasted_iota(jnp.int32, (rows, 2 * head_dim), 1) < head_dim
    parts = [
        jnp.where(low, columns[:, h : h + 1], columns[:, h + 1 : h + 2]) for h in range(0, HEADS, 2)
    ]
    return jnp.concatenate(parts, axis=1)


def cumul_rows(decay):
    shape = (GROUP, GROUP)
    upto = lax.broadcasted_iota(jnp.int32, shape, 0) <= lax.broadcasted_iota(jnp.int32, shape, 1)
    upto = jnp.where(upto, 1.0, 0.0).astype(bf16)
    high = decay.astype(bf16)
    rest = decay - high.astype(f32)
    middle = rest.astype(bf16)
    low = (rest - middle.astype(f32)).astype(bf16)
    return (
        jnp.dot(low, upto, preferred_element_type=f32)
        + jnp.dot(middle, upto, preferred_element_type=f32)
        + jnp.dot(high, upto, preferred_element_type=f32)
    )


def two_parts(x):
    high = x.astype(bf16)
    return high, (x - high.astype(f32)).astype(bf16)


def pair_weights(grad):
    low = lax.broadcasted_iota(jnp.int32, grad.shape, 1) < grad.shape[1] // 2
    none = jnp.zeros_like(grad)
    return jnp.concatenate([jnp.where(low, grad, none), jnp.where(low, none, grad)], axis=0)


def state_kernel(
    grad_ref, bc_ref, decay_ref, carried_ref, after_ref, cumul_ref, end_ref
):
    events, width = grad_ref.shape
    blocks = events // GROUP
    two = 2 * width // HEADS
    cumul = cumul_rows(
        jnp.concatenate([decay_ref[:, b * GROUP : (b + 1) * GROUP] for b in range(blocks)], axis=0)
    )
    cumul_ref[...] = cumul
    grown = jnp.exp(cumul)
    low = lax.broadcasted_iota(jnp.int32, (1, two), 1) < two // 2
    state = jnp.zeros((STATE, width), f32)
    log = jnp.zeros((1, width), f32)
    for b in range(blocks - 1, -1, -1):
        at = pl.ds(b * GROUP, GROUP)
        c = jnp.transpose(bc_ref[at, :].astype(f32))[STATE:, :]
        ends, log_end = [], []
        for h in range(0, HEADS, 2):
            high, rest = [], []
            for k in (b * HEADS + h, b * HEADS + h + 1):
                one, other = two_parts(c * grown[k : k + 1, :])
                high.append(one)
                rest.append(other)
            scaled = jnp.concatenate(
                [jnp.concatenate(high, axis=1), jnp.concatenate(rest, axis=1)], axis=0
            )
            grad = grad_ref[at, h // 2 * two : (h // 2 + 1) * two]
            both = jnp.dot(scaled, pair_weights(grad), preferred_element_type=f32)
            ends.append(both[:STATE, :] + both[STATE:, :])
            last = cumul[b * HEADS + h : b * HEADS + h + 2, GROUP - 1 :]
            log_end.append(jnp.where(low, last[:1, :], last[1:, :]))
        carried_ref[b] = state
        after_ref[b] = log
        log_end = jnp.concatenate(log_end, axis=1)
        state = jnp.concatenate(ends, axis=1) + jnp.exp(log_end) * state
        log = log + log_end
    end_ref[:STATE, :] = state
    end_ref[STATE:, :] = jnp.broadcast_to(log, (8, width))


def state_of(grad, bc, decay):
    events, width = grad.shape
    blocks = events // GROUP
    return pl.pallas_call(
        state_kernel,
        out_shape=[
            jax.ShapeDtypeStruct((blocks, STATE, width), f32),
            jax.ShapeDtypeStruct((blocks, 1, width), f32),
            jax.ShapeDtypeStruct((blocks * HEADS, GROUP), f32),
            jax.ShapeDtypeStruct((STATE + 8, width), f32),
        ],
        compiler_params=params(),
        cost_estimate=cost(4 * events * width * STATE, 4 * events * width),
        name="state",
    )(grad, bc, decay)


def local_kernel(
    grad_ref, bc_ref, cumul_ref, skip_ref, carried_ref, after_ref, _, out_ref, fade_ref
):
    width = grad_ref.shape[1]
    two = 2 * width // HEADS
    half = GROUP // 2
    shape = (half, half)
    later = lax.broadcasted_iota(jnp.int32, shape, 1) >= lax.broadcasted_iota(jnp.int32, shape, 0)
    low = lax.broadcasted_iota(jnp.int32, (GROUP, two), 1) < two // 2
    rows = cumul_ref[...]
    columns = jnp.transpose(rows)
    for block in range(grad_ref.shape[0] // GROUP):
        at = pl.ds(block * GROUP, GROUP)
        past = jnp.exp(after_ref[block])
        b, c = bc_ref[at, :STATE], bc_ref[at, STATE:]
        scores = lax.dot_general(b, c, (((1,), (1,)), ((), ())), preferred_element_type=f32)
        first = jnp.where(later, scores[:half, :half], 0.0)
        across = scores[:half, half:]
        last = jnp.where(later, scores[half:, half:], 0.0)
        high, rest = two_parts(carried_ref[block])
        carried = jnp.dot(b, high, preferred_element_type=f32) + jnp.dot(
            b, rest, preferred_element_type=f32
        )
        for h in range(0, HEADS, 2):
            span = slice(h // 2 * two, (h // 2 + 1) * two)
            grad = grad_ref[at, span]
            weights = pair_weights(grad)
            upper, lower, wide, ends = [], [], [], []
            for k in (block * HEADS + h, block * HEADS + h + 1):
                row = rows[k : k + 1, :]
                column = jnp.broadcast_to(columns[:, k : k + 1], (GROUP, two))
                near = jnp.exp(jnp.minimum(row[:, :half] - column[:half, :], 0.0)) * first
                far = jnp.exp(row[:, half:] - column[:half, :]) * across
                end = jnp.exp(jnp.minimum(row[:, half:] - column[half:, :], 0.0)) * last
                upper += [near.astype(bf16), far.astype(bf16)]
                lower.append(end.astype(bf16))
                wide.append(row[:, GROUP - 1 :] - column)
            inner = jnp.concatenate(
                [
                    jnp.dot(
                        jnp.concatenate(upper, axis=1), weights, preferred_element_type=f32
                    ),
                    jnp.dot(
                        jnp.concatenate(lower, axis=1),
                        jnp.concatenate([weights[half:GROUP], weights[GROUP + half :]], axis=0),
                        preferred_element_type=f32,
                    ),
                ],
                axis=0,
            )
            fading = jnp.exp(jnp.where(low, wide[0], wide[1]))
            gain = jnp.where(low[:1, :], skip_ref[:, h : h + 1], skip_ref[:, h + 1 : h + 2])
            out_ref[at, span] = inner + carried[:, span] * fading + gain * grad.astype(f32)
            fade_ref[at, span] = fading * past[:, span]


def local_rows(grad, bc, cumul, skip, carried, after, earlier):
    events, width = grad.shape
    blocks = events // GROUP
    at = lambda i: (i, 0)
    step = 2
    return pl.pallas_call(
        local_kernel,
        grid=(blocks // step,),
        in_specs=[
            pl.BlockSpec((step * GROUP, width), at),
            pl.BlockSpec((step * GROUP, 2 * STATE), at),
            pl.BlockSpec((step * HEADS, GROUP), at),
            pl.BlockSpec((1, HEADS), lambda i: (0, 0)),
            pl.BlockSpec((step, STATE, width), lambda i: (i, 0, 0)),
            pl.BlockSpec((step, 1, width), lambda i: (i, 0, 0)),
            pl.BlockSpec(memory_space=pl.ANY),
        ],
        out_specs=[
            pl.BlockSpec((step * GROUP, width), at), pl.BlockSpec((step * GROUP, width), at)
        ],
        out_shape=[
            jax.ShapeDtypeStruct((events, width), f32),
            jax.ShapeDtypeStruct((events, width), f32),
        ],
        compiler_params=params(),
        cost_estimate=cost(
            blocks * GROUP * GROUP * (2 * width + 8 * HEADS), 10 * events * width,
            blocks * GROUP * GROUP * HEADS,
        ),
        name="local",
    )(grad, bc, cumul, skip, carried, after, earlier)


def slots_kernel(owner_ref, row_ref, place_ref, starts_ref, ids_ref):
    holders, _, capacity = ids_ref.shape
    spans = [slice(k * GROUP, (k + 1) * GROUP) for k in range(owner_ref.shape[1] // GROUP)]
    shape = (GROUP, GROUP)
    before = lax.broadcasted_iota(jnp.int32, shape, 0) < lax.broadcasted_iota(jnp.int32, shape, 1)
    before = jnp.where(before, 1.0, 0.0).astype(bf16)
    ones = jnp.ones((8, GROUP), bf16)
    count = jnp.zeros((holders, 1), f32)
    count_row = jnp.zeros((8, holders), f32)
    names = lax.broadcasted_iota(jnp.int32, (holders, GROUP), 0)
    ranks = lax.broadcasted_iota(jnp.int32, (capacity, GROUP), 0)
    high = jnp.zeros((holders, capacity), f32)
    low = jnp.zeros((holders, capacity), f32)
    across = (((1,), (1,)), ((), ()))
    hits_of, rank_of = [], []
    for at in spans:
        hits = jnp.where(names == owner_ref[:, at], 1.0, 0.0)
        hit = hits.astype(bf16)
        earlier = jnp.dot(hit, before, preferred_element_type=f32) + count
        rank = jnp.sum(hits * earlier, axis=0, keepdims=True)
        count = count + jnp.sum(hits, axis=1, keepdims=True)
        count_row = count_row + lax.dot_general(ones, hit, across, preferred_element_type=f32)
        hits_of.append(hits)
        rank_of.append(rank)
        ranked = jnp.where(ranks == rank.astype(jnp.int32), 1.0, 0.0).astype(bf16)
        named = row_ref[:, at] + 1
        upper = (hits * (named // 64).astype(f32)).astype(bf16)
        lower = (hits * (named % 64).astype(f32)).astype(bf16)
        high = high + lax.dot_general(upper, ranked, across, preferred_element_type=f32)
        low = low + lax.dot_general(lower, ranked, across, preferred_element_type=f32)
    ids_ref[:, 0, :] = (high * 64.0 + low).astype(jnp.int32)

    whole = lambda n: jnp.floor((n + (ALIGN - 1)) * (1.0 / ALIGN))
    square = (holders, holders)
    one = lax.broadcasted_iota(jnp.int32, square, 0)
    two = lax.broadcasted_iota(jnp.int32, square, 1)
    column = jnp.broadcast_to(whole(count), (holders, 128)).astype(bf16)
    sooner = jnp.where(two < one, 1.0, 0.0).astype(bf16)
    base = jnp.dot(sooner, column, preferred_element_type=f32)[:, :1] * ALIGN
    sooner = jnp.where(one < two, 1.0, 0.0).astype(bf16)
    starts = jnp.dot(whole(count_row).astype(bf16), sooner, preferred_element_type=f32) * ALIGN
    starts_ref[...] = starts[:1, :].astype(jnp.int32)
    for at, hits, rank in zip(spans, hits_of, rank_of):
        place = jnp.sum(hits * base, axis=0, keepdims=True) + rank
        place_ref[:, at] = place.astype(jnp.int32)


def slots(owner, row, holders, capacity):
    return pl.pallas_call(
        slots_kernel,
        out_shape=[
            jax.ShapeDtypeStruct(owner.shape, jnp.int32),
            jax.ShapeDtypeStruct((1, holders), jnp.int32),
            jax.ShapeDtypeStruct((holders, 1, capacity), jnp.int32),
        ],
        compiler_params=params(),
        cost_estimate=cost(2 * holders * owner.size * (GROUP + 2 * capacity), 8 * owner.size),
        name="slots",
    )(owner, row)


def send_kernel(
    blocks, tiles, sides_ref, starts_ref, place_ref, bc_ref, local_ref, fade_ref, end_ref, *refs,
):
    hops, (_, out_ref, high, low, rows, ordered, done) = refs[:-7], refs[-7:]
    step = pl.program_id(0)
    events, width = rows.shape
    block = events // blocks
    holders = starts_ref.shape[1]
    capacity = out_ref.shape[0] // holders
    tile = (ordered.shape[0] - capacity) // tiles

    @pl.when(step == 0)
    def _():
        state = jnp.zeros((STATE, width), f32)
        for hop in hops[::-1]:
            state = hop[:STATE, :] + jnp.exp(hop[STATE : STATE + 1, :]) * state
        through = end_ref[:STATE, :] + jnp.exp(end_ref[STATE : STATE + 1, :]) * state
        high[...], low[...] = two_parts(jnp.where(sides_ref[0] == 0, through, state))
        ordered[tiles * tile :, :] = jnp.zeros((capacity, width), bf16)

    @pl.when(step < blocks)
    def _():
        b = bc_ref[:, :STATE]
        part = jnp.dot(b, high[...], preferred_element_type=f32) + jnp.dot(
            b, low[...], preferred_element_type=f32
        )
        row = (local_ref[...] + part * fade_ref[...]).astype(bf16)
        rows[pl.ds(pl.multiple_of(step * block, block), block), :] = row

    @pl.when(step >= blocks)
    def _():
        first = pl.multiple_of((step - blocks) * tile, tile)
        names = lax.broadcasted_iota(jnp.int32, (tile, events), 0) + first
        chosen = jnp.where(names == place_ref[...], 1.0, 0.0).astype(bf16)
        ordered[pl.ds(first, tile), :] = jnp.dot(
            chosen, rows[...], preferred_element_type=f32
        ).astype(bf16)

    @pl.when(step == blocks + tiles - 1)
    def _():
        def copy(k):
            start = pl.multiple_of(starts_ref[0, k], ALIGN)
            return pltpu.make_async_copy(
                ordered.at[pl.ds(start, capacity), :],
                out_ref.at[pl.ds(k * capacity, capacity), :],
                done.at[k],
            )

        for k in range(holders):
            copy(k).start()
        for k in range(holders):
            copy(k).wait()


def sent_rows(sides, starts, place, bc, local, fade, partner, hops, capacity, earlier):
    events, width = local.shape
    holders = starts.shape[1]
    blocks, tiles = 4, 4
    block = events // blocks
    ordered = -(-(events + (ALIGN - 1) * holders) // (tiles * ALIGN)) * tiles * ALIGN
    whole = lambda a: pl.BlockSpec(a.shape, lambda i: (0,) * a.ndim)
    at = lambda i: (jnp.minimum(i, blocks - 1), 0)
    smem = pl.BlockSpec(memory_space=pltpu.SMEM)
    return pl.pallas_call(
        functools.partial(send_kernel, blocks, tiles),
        grid=(blocks + tiles,),
        in_specs=[
            smem,
            smem,
            whole(place),
            pl.BlockSpec((block, 2 * STATE), at),
            pl.BlockSpec((block, width), at),
            pl.BlockSpec((block, width), at),
            whole(partner),
        ]
        + [whole(hop) for hop in hops]
        + [pl.BlockSpec(memory_space=pl.ANY)],
        out_specs=pl.BlockSpec(memory_space=pl.ANY),
        out_shape=jax.ShapeDtypeStruct((holders * capacity, width), bf16),
        scratch_shapes=[
            pltpu.VMEM((STATE, width), bf16),
            pltpu.VMEM((STATE, width), bf16),
            pltpu.VMEM((events, width), bf16),
            pltpu.VMEM((ordered + capacity, width), bf16),
            pltpu.SemaphoreType.DMA((holders,)),
        ],
        compiler_params=params(),
        cost_estimate=cost(2 * ordered * events * width, 12 * events * width),
        name="send",
    )(sides, starts, place, bc, local, fade, partner, *hops, earlier)


def update_kernel(tile, ids_ref, got_ref, table_ref, accum_ref, new_table_ref, new_accum_ref):
    parts, lanes = ids_ref.shape
    ids = jnp.concatenate([ids_ref[k : k + 1, :] for k in range(parts)], axis=1)
    names = lax.broadcasted_iota(jnp.int32, (tile, parts * lanes), 0)
    names = names + (pl.program_id(0) * tile + 1)
    chosen = jnp.where(names == ids, 1.0, 0.0).astype(bf16)
    total = jnp.dot(chosen, got_ref[...], preferred_element_type=f32)
    accum = accum_ref[...] + total * total
    new_accum_ref[...] = accum
    new_table_ref[...] = (
        table_ref[...].astype(f32) - learn_rate * total * lax.rsqrt(accum)
    ).astype(bf16)


def updated(ids, got, table, accum):
    owned, width = table.shape
    tile = 512
    block = pl.BlockSpec((tile, width), lambda i: (i, 0))
    whole = lambda a: pl.BlockSpec(a.shape, lambda i: (0, 0))
    return pl.pallas_call(
        functools.partial(update_kernel, tile),
        grid=(owned // tile,),
        in_specs=[whole(ids), whole(got), block, block],
        out_specs=[block] * 2,
        out_shape=[
            jax.ShapeDtypeStruct(table.shape, bf16),
            jax.ShapeDtypeStruct(accum.shape, f32),
        ],
        compiler_params=params(),
        cost_estimate=cost(2 * owned * got.shape[0] * width, 12 * owned * width),
        name="update",
    )(ids, got, table, accum)


def pair_kernel(sides_ref, end_ref, partner_ref, _, pair_ref):
    first = sides_ref[0] == 0
    end, partner = end_ref[...], partner_ref[...]
    early = jnp.where(first, end, partner)
    late = jnp.where(first, partner, end)
    fade = jnp.exp(early[STATE : STATE + 1, :])
    pair_ref[:STATE, :] = early[:STATE, :] + fade * late[:STATE, :]
    pair_ref[STATE:, :] = early[STATE:, :] + late[STATE:, :]


def pair_state(sides, end, partner, earlier):
    vmem = pl.BlockSpec(memory_space=pltpu.VMEM)
    return pl.pallas_call(
        pair_kernel,
        in_specs=[
            pl.BlockSpec(memory_space=pltpu.SMEM), vmem, vmem, pl.BlockSpec(memory_space=pl.ANY)
        ],
        out_shape=jax.ShapeDtypeStruct(end.shape, f32),
        compiler_params=params(),
        cost_estimate=cost(4 * end.size, 12 * end.size),
        name="pair",
    )(sides, end, partner, earlier)


def on_device(out_grad, bc_proj, decay_log, skip_gain, owner, item_row, table, accum):
    users, events, width = out_grad.shape
    grad = out_grad.reshape(events, width)
    bc = bc_proj.reshape(events, 2 * STATE)
    decay = decay_log.reshape(HEADS, events)
    size = lax.axis_size("tm")
    holders = size * lax.axis_size("table")
    capacity = 2 * events // holders
    side = lax.axis_index("tm") % 2
    sides = jnp.broadcast_to(side, (1,)).astype(jnp.int32)

    place, starts, ids = slots(owner.reshape(1, events), item_row, holders, capacity)
    got_ids = lax.all_to_all(ids, BOTH, split_axis=0, concat_axis=0, tiled=True)
    carried, after, cumul, end = state_of(grad, bc, decay)
    partner = lax.ppermute(end, "tm", [(i, i ^ 1) for i in range(size)])
    pair = pair_state(sides, end, partner, place)
    hops = [
        lax.ppermute(pair, "tm", [(i, i - k) for i in range(k, size)]) for k in range(2, size, 2)
    ]
    local, fade = local_rows(
        grad, bc, cumul, skip_gain.reshape(1, HEADS), carried, after, pair
    )
    rows = sent_rows(
        sides, starts, place, bc, local, fade, partner, hops, capacity, got_ids
    )
    got = lax.all_to_all(
        rows.reshape(holders, capacity, width), BOTH, split_axis=0, concat_axis=0, tiled=True
    ).reshape(holders * capacity, width)
    return updated(got_ids.reshape(-1, 128), got, table, accum)


def solution(mesh):
    placed = (
        P("table", "tm", None),
        P("table", "tm", None),
        P("table", None, "tm"),
        P(),
        P("table", "tm", None),
        P("table", "tm"),
        P(("tm", "table"), None),
        P(("tm", "table"), None),
    )
    return jax.shard_map(
        on_device,
        mesh=mesh,
        in_specs=placed,
        out_specs=(P(("tm", "table"), None), P(("tm", "table"), None)),
        check_vma=False,
    )
```

time: 191 us -> 162 us (0.85)
  waiting for transfers between devices: 93.2 us -> 1 us
  blocking collectives: 16 us -> 99.6 us
  local copies, waits for them, and re-layouts: 11.4 us -> 1.37 us
  other arithmetic: 5.03 us -> 0 us
  Pallas kernels: 48.5 us -> 44.2 us
    all_to_all x2 -> x0, waiting for transfers between devices: 93.2 us -> none  [the longest x1 93.2 us: on_device(): lax.all_to_all(rows.reshape(holders, capacity, width), BOTH, split_axis=0...]
    all_to_all x1, blocking collectives: 16 us -> 99.6 us  [on_device(): lax.all_to_all(rows.reshape(holders, capacity, width), BOTH, split_axis=0...]
    all_to_all x2 -> x0, starting transfers between devices: 9.55 us -> none  [the longest x1 5.96 us: on_device(): lax.all_to_all(rows.reshape(holders, capacity, width), BOTH, split_axis=0...]
    unnamed x31 -> x10, local copies, waits for them, and re-layouts: 10.8 us -> 1.37 us
    ppermute x0 -> x4, starting transfers between devices: none -> 6.83 us  [the longest x3 3.86 us: on_device(): lax.ppermute(pair, 'tm', [(i, i - k) for i in range(k, size)])]
    unnamed x7 -> x0, other arithmetic: 4.35 us -> none
    pallas_call x4 -> x5, Pallas kernels: 37.2 us -> 33 us  [the longest x1 13.9 us: sent_rows(): pl.pallas_call(functools.partial(send_kernel, blocks, tiles), grid=(block...]
    all_to_all x1, starting transfers between devices: 5.99 us -> 8.1 us  [on_device(): got_ids = lax.all_to_all(ids, BOTH, split_axis=0, concat_axis=0, tiled=True)]
  transfers between devices with their start and end apart: 3 -> 5, of which waited for: 1 -> 1; matrix products, arithmetic and copies ran while one was open for 1% -> 0% of each run, Pallas kernels for 7% -> 8%
where the time goes in v2:
time: 162 us
  blocking collectives  99.6 us (61%)
  Pallas kernels  44.2 us (27%)
  starting transfers between devices  14.9 us (9%)
    all_to_all x1, blocking collectives, on_device(): lax.all_to_all(rows.reshape(holders, capacity, width), BOTH, split_axis=0...  99.6 us
    pallas_call x1, Pallas kernels, sent_rows(): pl.pallas_call(functools.partial(send_kernel, blocks, tiles), grid=(block...  13.9 us
    pallas_call x1, Pallas kernels, updated(): pl.pallas_call(functools.partial(update_kernel, tile), grid=(owned // til...  11.2 us
    pallas_call x1, Pallas kernels, local_rows(): pl.pallas_call(local_kernel, grid=(blocks // step,), in_specs=[pl.BlockSp...  9.97 us
    all_to_all x1, starting transfers between devices, on_device(): got_ids = lax.all_to_all(ids, BOTH, split_axis=0, concat_axis=0, tiled=True)  8.1 us
    pallas_call x1, Pallas kernels, state_of(): pl.pallas_call(state_kernel, out_shape=[jax.ShapeDtypeStruct((blocks, STA...  4.42 us
    ppermute x3, starting transfers between devices, on_device(): lax.ppermute(pair, 'tm', [(i, i - k) for i in range(k, size)])  3.86 us
  transfers between devices with their start and end apart: 5, of which 1 were waited for; matrix products, arithmetic and copies ran while one was open for 0% of the time, Pallas kernels for 8%

profile of v2, /device:TPU:0, one launch (start us, length us, event | category | flops | bytes accessed | tf_op | source)
XLA Modules:
  0.0 161.8 jit_solution(1357700298898025528)
XLA Ops:
  0.6 4.4 %state.1 = (f32[8,64,512]{2,1,0:T(8,128)}, f32[8,1,512]{2,1,0:T(1,128)}, f32[64,256]{1,0:T(8,128)}, f32[72,512]{1,0:T(8,128)}) custom-call(bf16[2048,512]{1,0:T(8,128)(2,1)} %bitcast.11, bf16[2048,128]{1,0:T(8,128)(2,1)} %bitcast.13, f32[8,2048]{1,0:T(8,128)} %bitcast.16), custom_call_target="tpu_custom_call" | custom-call | flops 268435456 | bytes 4194304 | tf_op jit(solution)/shard_map/state/pallas_call | solution.py:111
  5.0 3.0 %collective-permute-start = (f32[72,512]{1,0:T(8,128)}, f32[72,512]{1,0:T(8,128)S(1)}, u32[]{:S(2)}, u32[]{:S(2)}) collective-permute-start(f32[72,512]{1,0:T(8,128)} %get-tuple-element.17.end_ref), channel_id=1, source_target_pairs={{0,4},{4,0},{8,12},{12,8},{16,20},{20,16},{24,28},{28,24},{1,5},{5... | collective-permute-start | bytes 442376 | tf_op jit(solution)/shard_map/ppermute | solution.py:439
  8.0 3.1 %slots.1 = (s32[1,2048]{1,0:T(1,128)}, s32[1,32]{1,0:T(1,128)}, s32[32,1,128]{2,1,0:T(1,128)}) custom-call(s32[1,2048]{1,0:T(1,128)} %bitcast.18, s32[1,2048]{1,0:T(1,128)} %row_ref.1), custom_call_target="tpu_custom_call" | custom-call | flops 67108864 | bytes 16384 | tf_op jit(solution)/shard_map/slots/pallas_call | solution.py:262
  11.1 1.0 collective-permute-done.partner_ref.end_ref
  12.1 0.0 copy-start
  12.1 0.7 copy-done
  12.7 1.7 %pair.1._ = f32[72,512]{1,0:T(8,128)} custom-call(s32[1]{0:T(128)} %bitcast.2.sides_ref, f32[72,512]{1,0:T(8,128)} %get-tuple-element.17.end_ref, f32[72,512]{1,0:T(8,128)} %copy-done, s32[1,2048]{1,0:T(1,128)} %get-tuple-element.13._.place_ref), custom_call_target="tpu_custom_call" | custom-call | flops 147456 | bytes 442368 | tf_op jit(solution)/shard_map/pair/pallas_call | solution.py:413
  14.4 1.3 collective-permute-start.3
  15.7 1.3 collective-permute-start.2
  17.0 1.3 collective-permute-start.1
  18.3 8.1 %all-to-all-start = ((s32[32,1,128]{2,1,0:T(1,128)}), s32[32,1,128]{2,1,0:T(1,128)S(1)}, u32[]{:S(2)}, u32[]{:S(2)}) async-start(s32[32,1,128]{2,1,0:T(1,128)} %get-tuple-element.11), calls=%async_computation | async-start | bytes 32768 | tf_op jit(solution)/shard_map/all_to_all | solution.py:437
  26.4 10.0 %local.1 = (f32[2048,512]{1,0:T(8,128)}, f32[2048,512]{1,0:T(8,128)}) custom-call(bf16[2048,512]{1,0:T(8,128)(2,1)} %bitcast.12, bf16[2048,128]{1,0:T(8,128)(2,1)} %bitcast.14, f32[64,256]{1,0:T(8,128)} %get-tuple-element.14.cumul_ref, f32[1,8]{1,0:T(1,128)} %bitcast.19, f32[8,64,512]{2,1,0:T(8,128)} %get-tuple-element.15.carried_ref, ...), custom_call_target="tpu_custom_call" | custom-call | flops 570425344 | bytes 10485760 | tf_op jit(solution)/shard_map/local/pallas_call | solution.py:186
  36.4 0.0 all-to-all-done.refs_3_
  36.4 0.0 copy-start.1
  36.4 0.0 collective-permute-done.3.refs_2_
  36.4 0.0 copy-start.2
  36.4 0.0 collective-permute-done.2.refs_1_
  36.4 0.0 copy-start.3
  36.4 0.0 collective-permute-done.1.refs_0_
  36.4 0.0 copy-start.4
  36.5 0.5 copy-done.1
  37.0 0.1 copy-done.2
  37.1 0.0 copy-done.3
  37.1 0.0 copy-done.4
  37.2 13.9 %send.1 = bf16[4096,512]{1,0:T(8,128)(2,1)} custom-call(s32[1]{0:T(128)} %bitcast.2.sides_ref, s32[1,32]{1,0:T(1,128)} %get-tuple-element.12.starts_ref, s32[1,2048]{1,0:T(1,128)} %get-tuple-element.13._.place_ref, bf16[2048,128]{1,0:T(8,128)(2,1)} %bitcast.15, f32[2048,512]{1,0:T(8,128)} %get-tuple-element.18.local_ref, ...), custom_call_target="tpu_custom_call" | custom-call | flops 5368709120 | bytes 12582912 | tf_op jit(solution)/shard_map/send/pallas_call | solution.py:338
  51.1 99.6 %all_to_all.10 = bf16[32,128,512]{2,1,0:T(8,128)(2,1)} all-to-all(bf16[32,128,512]{2,1,0:T(8,128)(2,1)} %bitcast.9), channel_id=1, replica_groups=mesh['tm'=8,'table'=4] {'tm','table'}, dimensions={0} | all-to-all | bytes 8388608 | tf_op jit(solution)/shard_map/all_to_all | solution.py:450
  150.7 11.2 %update.1 = (bf16[1536,512]{1,0:T(8,128)(2,1)}, f32[1536,512]{1,0:T(8,128)}) custom-call(s32[32,128]{1,0:T(8,128)} %bitcast.17, bf16[4096,512]{1,0:T(8,128)(2,1)} %bitcast.10, bf16[1536,512]{1,0:T(8,128)(2,1)} %table_ref.1, f32[1536,512]{1,0:T(8,128)} %accum_ref.1), custom_call_target="tpu_custom_call" | custom-call | flops 6442450944 | bytes 9437184 | tf_op jit(solution)/shard_map/update/pallas_call | solution.py:386
Async XLA Ops:
  5.0 7.0 %collective-permute-start = (f32[72,512]{1,0:T(8,128)}, f32[72,512]{1,0:T(8,128)S(1)}, u32[]{:S(2)}, u32[]{:S(2)}) collective-permute-start(f32[72,512]{1,0:T(8,128)} %get-tuple-element.17.end_ref), channel_id=1, source_target_pairs={{0,4},{4,0},{8,12},{12,8},{16,20},{20,16},{24,28},{28,24},{1,5},{5... | collective-permute-start | bytes 442376 | tf_op jit(solution)/shard_map/ppermute | solution.py:439
  12.1 0.7 copy-start
  14.4 22.0 %collective-permute-start.3 = (f32[72,512]{1,0:T(8,128)}, f32[72,512]{1,0:T(8,128)S(1)}, u32[]{:S(2)}, u32[]{:S(2)}) collective-permute-start(f32[72,512]{1,0:T(8,128)} %pair.1._), channel_id=1, source_target_pairs={{24,0},{28,4},{25,1},{29,5},{26,2},{30,6},{27,3},{31,7}} | collective-permute-start | bytes 442376 | tf_op jit(solution)/shard_map/ppermute | solution.py:442
  15.7 20.7 %collective-permute-start.2 = (f32[72,512]{1,0:T(8,128)}, f32[72,512]{1,0:T(8,128)S(1)}, u32[]{:S(2)}, u32[]{:S(2)}) collective-permute-start(f32[72,512]{1,0:T(8,128)} %pair.1._), channel_id=1, source_target_pairs={{16,0},{20,4},{24,8},{28,12},{17,1},{21,5},{25,9},{29,13},{18,2},{... | collective-permute-start | bytes 442376 | tf_op jit(solution)/shard_map/ppermute | solution.py:442
  17.0 19.4 %collective-permute-start.1 = (f32[72,512]{1,0:T(8,128)}, f32[72,512]{1,0:T(8,128)S(1)}, u32[]{:S(2)}, u32[]{:S(2)}) collective-permute-start(f32[72,512]{1,0:T(8,128)} %pair.1._), channel_id=1, source_target_pairs={{8,0},{12,4},{16,8},{20,12},{24,16},{28,20},{9,1},{13,5},{17,9},{2... | collective-permute-start | bytes 442376 | tf_op jit(solution)/shard_map/ppermute | solution.py:442
  18.3 18.1 %all-to-all-start = ((s32[32,1,128]{2,1,0:T(1,128)}), s32[32,1,128]{2,1,0:T(1,128)S(1)}, u32[]{:S(2)}, u32[]{:S(2)}) async-start(s32[32,1,128]{2,1,0:T(1,128)} %get-tuple-element.11), calls=%async_computation | async-start | bytes 32768 | tf_op jit(solution)/shard_map/all_to_all | solution.py:437
  36.4 0.6 copy-start.1
  36.4 0.7 copy-start.2
  36.4 0.7 copy-start.3
  36.4 0.7 copy-start.4

commit v3 on v2

--- a/solution.py
+++ b/solution.py
@@ -11,6 +11,8 @@
 STATE = 64
 GROUP = 256
 ALIGN = 16
+PARTS = 2
+PART_HEADS = HEADS // PARTS
 BOTH = ("tm", "table")
 VMEM_BYTES = 60 * 1024 * 1024
 
@@ -26,16 +28,6 @@
 
 def cost(flops, moved, exps=0):
     return pl.CostEstimate(flops=flops, bytes_accessed=moved, transcendentals=exps)
-
-
-def spread(columns, width):
-    rows = columns.shape[0]
-    head_dim = width // HEADS
-    low = lax.broadcasted_iota(jnp.int32, (rows, 2 * head_dim), 1) < head_dim
-    parts = [
-        jnp.where(low, columns[:, h : h + 1], columns[:, h + 1 : h + 2]) for h in range(0, HEADS, 2)
-    ]
-    return jnp.concatenate(parts, axis=1)
 
 
 def cumul_rows(decay):
@@ -123,10 +115,10 @@
 
 
 def local_kernel(
-    grad_ref, bc_ref, cumul_ref, skip_ref, carried_ref, after_ref, _, out_ref, fade_ref
+    part, grad_ref, bc_ref, cumul_ref, skip_ref, carried_ref, after_ref, _, out_ref, fade_ref
 ):
     width = grad_ref.shape[1]
-    two = 2 * width // HEADS
+    two = 2 * width // PART_HEADS
     half = GROUP // 2
     shape = (half, half)
     later = lax.broadcasted_iota(jnp.int32, shape, 1) >= lax.broadcasted_iota(jnp.int32, shape, 0)
@@ -145,12 +137,13 @@
         carried = jnp.dot(b, high, preferred_element_type=f32) + jnp.dot(
             b, rest, preferred_element_type=f32
         )
-        for h in range(0, HEADS, 2):
+        for h in range(0, PART_HEADS, 2):
+            head = part * PART_HEADS + h
             span = slice(h // 2 * two, (h // 2 + 1) * two)
             grad = grad_ref[at, span]
             weights = pair_weights(grad)
             upper, lower, wide, ends = [], [], [], []
-            for k in (block * HEADS + h, block * HEADS + h + 1):
+            for k in (block * HEADS + head, block * HEADS + head + 1):
                 row = rows[k : k + 1, :]
                 column = jnp.broadcast_to(columns[:, k : k + 1], (GROUP, two))
                 near = jnp.exp(jnp.minimum(row[:, :half] - column[:half, :], 0.0)) * first
@@ -173,26 +166,27 @@
                 axis=0,
             )
             fading = jnp.exp(jnp.where(low, wide[0], wide[1]))
-            gain = jnp.where(low[:1, :], skip_ref[:, h : h + 1], skip_ref[:, h + 1 : h + 2])
+            gain = jnp.where(low[:1, :], skip_ref[:, head : head + 1], skip_ref[:, head + 1 : head + 2])
             out_ref[at, span] = inner + carried[:, span] * fading + gain * grad.astype(f32)
             fade_ref[at, span] = fading * past[:, span]
 
 
-def local_rows(grad, bc, cumul, skip, carried, after, earlier):
-    events, width = grad.shape
+def local_rows(part, grad, bc, cumul, skip, carried, after, earlier):
+    events = grad.shape[0]
+    width = grad.shape[1] // PARTS
     blocks = events // GROUP
     at = lambda i: (i, 0)
-    step = 2
+    step = 4
     return pl.pallas_call(
-        local_kernel,
+        functools.partial(local_kernel, part),
         grid=(blocks // step,),
         in_specs=[
-            pl.BlockSpec((step * GROUP, width), at),
+            pl.BlockSpec((step * GROUP, width), lambda i: (i, part)),
             pl.BlockSpec((step * GROUP, 2 * STATE), at),
             pl.BlockSpec((step * HEADS, GROUP), at),
             pl.BlockSpec((1, HEADS), lambda i: (0, 0)),
-            pl.BlockSpec((step, STATE, width), lambda i: (i, 0, 0)),
-            pl.BlockSpec((step, 1, width), lambda i: (i, 0, 0)),
+            pl.BlockSpec((step, STATE, width), lambda i: (i, 0, part)),
+            pl.BlockSpec((step, 1, width), lambda i: (i, 0, part)),
             pl.BlockSpec(memory_space=pl.ANY),
         ],
         out_specs=[
@@ -326,10 +320,10 @@
             copy(k).wait()
 
 
-def sent_rows(sides, starts, place, bc, local, fade, partner, hops, capacity, earlier):
+def sent_rows(part, sides, starts, place, bc, local, fade, partner, hops, capacity, earlier):
     events, width = local.shape
     holders = starts.shape[1]
-    blocks, tiles = 4, 4
+    blocks, tiles = 2, 1
     block = events // blocks
     ordered = -(-(events + (ALIGN - 1) * holders) // (tiles * ALIGN)) * tiles * ALIGN
     whole = lambda a: pl.BlockSpec(a.shape, lambda i: (0,) * a.ndim)
@@ -345,11 +339,10 @@
             pl.BlockSpec((block, 2 * STATE), at),
             pl.BlockSpec((block, width), at),
             pl.BlockSpec((block, width), at),
-            whole(partner),
         ]
-        + [whole(hop) for hop in hops]
+        + [pl.BlockSpec((hop.shape[0], width), lambda i: (0, part)) for hop in (partner, *hops)]
         + [pl.BlockSpec(memory_space=pl.ANY)],
-        out_specs=pl.BlockSpec(memory_space=pl.ANY),
+        out_specs=pl.BlockSpec(memory_space=pltpu.HBM),
         out_shape=jax.ShapeDtypeStruct((holders * capacity, width), bf16),
         scratch_shapes=[
             pltpu.VMEM((STATE, width), bf16),
@@ -364,7 +357,8 @@
     )(sides, starts, place, bc, local, fade, partner, *hops, earlier)
 
 
-def update_kernel(tile, ids_ref, got_ref, table_ref, accum_ref, new_table_ref, new_accum_ref):
+def update_kernel(tile, ids_ref, got_ref, table_ref, accum_ref, *refs):
+    new_table_ref, new_accum_ref = refs[-2:]
     parts, lanes = ids_ref.shape
     ids = jnp.concatenate([ids_ref[k : k + 1, :] for k in range(parts)], axis=1)
     names = lax.broadcasted_iota(jnp.int32, (tile, parts * lanes), 0)
@@ -378,48 +372,38 @@
     ).astype(bf16)
 
 
-def updated(ids, got, table, accum):
-    owned, width = table.shape
+def updated(part, ids, got, table, accum, before):
+    owned = table.shape[0]
+    width = got.shape[1]
     tile = 512
-    block = pl.BlockSpec((tile, width), lambda i: (i, 0))
+    block = pl.BlockSpec((tile, width), lambda i: (i, part))
     whole = lambda a: pl.BlockSpec(a.shape, lambda i: (0, 0))
     return pl.pallas_call(
         functools.partial(update_kernel, tile),
         grid=(owned // tile,),
-        in_specs=[whole(ids), whole(got), block, block],
+        in_specs=[whole(ids), whole(got), block, block]
+        + [pl.BlockSpec(memory_space=pl.ANY)] * len(before),
         out_specs=[block] * 2,
         out_shape=[
             jax.ShapeDtypeStruct(table.shape, bf16),
             jax.ShapeDtypeStruct(accum.shape, f32),
         ],
+        input_output_aliases={4 + k: k for k in range(len(before))},
         compiler_params=params(),
         cost_estimate=cost(2 * owned * got.shape[0] * width, 12 * owned * width),
         name="update",
-    )(ids, got, table, accum)
-
-
-def pair_kernel(sides_ref, end_ref, partner_ref, _, pair_ref):
-    first = sides_ref[0] == 0
-    end, partner = end_ref[...], partner_ref[...]
-    early = jnp.where(first, end, partner)
-    late = jnp.where(first, partner, end)
-    fade = jnp.exp(early[STATE : STATE + 1, :])
-    pair_ref[:STATE, :] = early[:STATE, :] + fade * late[:STATE, :]
-    pair_ref[STATE:, :] = early[STATE:, :] + late[STATE:, :]
-
-
-def pair_state(sides, end, partner, earlier):
-    vmem = pl.BlockSpec(memory_space=pltpu.VMEM)
-    return pl.pallas_call(
-        pair_kernel,
-        in_specs=[
-            pl.BlockSpec(memory_space=pltpu.SMEM), vmem, vmem, pl.BlockSpec(memory_space=pl.ANY)
-        ],
-        out_shape=jax.ShapeDtypeStruct(end.shape, f32),
-        compiler_params=params(),
-        cost_estimate=cost(4 * end.size, 12 * end.size),
-        name="pair",
-    )(sides, end, partner, earlier)
+    )(ids, got, table, accum, *before)
+
+
+def pair_state(side, end, partner):
+    early = jnp.where(side == 0, end, partner)
+    late = jnp.where(side == 0, partner, end)
+    return jnp.concatenate(
+        [
+            early[:STATE] + jnp.exp(early[STATE : STATE + 1]) * late[:STATE],
+            early[STATE:] + late[STATE:],
+        ]
+    )
 
 
 def on_device(out_grad, bc_proj, decay_log, skip_gain, owner, item_row, table, accum):
@@ -435,22 +419,29 @@
 
     place, starts, ids = slots(owner.reshape(1, events), item_row, holders, capacity)
     got_ids = lax.all_to_all(ids, BOTH, split_axis=0, concat_axis=0, tiled=True)
+    ids = got_ids.reshape(-1, 128)
+    skip = skip_gain.reshape(1, HEADS)
+
     carried, after, cumul, end = state_of(grad, bc, decay)
     partner = lax.ppermute(end, "tm", [(i, i ^ 1) for i in range(size)])
-    pair = pair_state(sides, end, partner, place)
+    place, partner = lax.optimization_barrier((place, partner))
+    pair = pair_state(side, end, partner)
     hops = [
         lax.ppermute(pair, "tm", [(i, i - k) for i in range(k, size)]) for k in range(2, size, 2)
     ]
-    local, fade = local_rows(
-        grad, bc, cumul, skip_gain.reshape(1, HEADS), carried, after, pair
-    )
-    rows = sent_rows(
-        sides, starts, place, bc, local, fade, partner, hops, capacity, got_ids
-    )
-    got = lax.all_to_all(
-        rows.reshape(holders, capacity, width), BOTH, split_axis=0, concat_axis=0, tiled=True
-    ).reshape(holders * capacity, width)
-    return updated(got_ids.reshape(-1, 128), got, table, accum)
+
+    new, earlier = (), pair
+    for part in range(PARTS):
+        local, fade = local_rows(part, grad, bc, cumul, skip, carried, after, earlier)
+        rows = sent_rows(
+            part, sides, starts, place, bc, local, fade, partner, hops, capacity, got_ids
+        )
+        got = lax.all_to_all(
+            rows.reshape(holders, capacity, -1), BOTH, split_axis=0, concat_axis=0, tiled=True
+        )
+        new = updated(part, ids, got.reshape(holders * capacity, -1), table, accum, new)
+        earlier = rows
+    return new
 
 
 def solution(mesh):

time: 162 us -> 156 us (0.963)
  blocking collectives: 99.6 us -> 0 us
  waiting for transfers between devices: 1 us -> 79.7 us
  starting transfers between devices: 14.9 us -> 23.7 us
  Pallas kernels: 44.2 us -> 48 us
    all_to_all x1 -> x0, blocking collectives: 99.6 us -> none  [on_device(): lax.all_to_all(rows.reshape(holders, capacity, width), BOTH, split_axis=0...]
    all_to_all x0 -> x2, waiting for transfers between devices: none -> 77.3 us  [on_device(): lax.all_to_all(rows.reshape(holders, capacity, -1), BOTH, split_axis=0, c...]
    all_to_all x0 -> x2, starting transfers between devices: none -> 8.78 us  [on_device(): lax.all_to_all(rows.reshape(holders, capacity, -1), BOTH, split_axis=0, c...]
    pallas_call x1 -> x2, Pallas kernels: 11.2 us -> 13.5 us  [updated(): pl.pallas_call(functools.partial(update_kernel, tile), grid=(owned // til...]
    pallas_call x1 -> x2, Pallas kernels: 13.9 us -> 14.9 us  [sent_rows(): pl.pallas_call(functools.partial(send_kernel, blocks, tiles), grid=(block...]
  transfers between devices with their start and end apart: 5 -> 7, of which waited for: 1 -> 4; matrix products, arithmetic and copies ran while one was open for 0% -> 0% of each run, Pallas kernels for 8% -> 14%
where the time goes in v3:
time: 156 us; the launch traced here: 155 us
  waiting for transfers between devices  79.7 us (51%)
  Pallas kernels  48 us (31%)
  starting transfers between devices  23.7 us (15%)
  local copies, waits for them, and re-layouts  2.1 us (1%)
    all_to_all x2, waiting for transfers between devices, on_device(): lax.all_to_all(rows.reshape(holders, capacity, -1), BOTH, split_axis=0, c...  77.3 us
    pallas_call x2, Pallas kernels, sent_rows(): pl.pallas_call(functools.partial(send_kernel, blocks, tiles), grid=(block...  14.9 us
    pallas_call x2, Pallas kernels, updated(): pl.pallas_call(functools.partial(update_kernel, tile), grid=(owned // til...  13.5 us
    pallas_call x2, Pallas kernels, local_rows(): pl.pallas_call(functools.partial(local_kernel, part), grid=(blocks // ste...  12.2 us
    all_to_all x2, starting transfers between devices, on_device(): lax.all_to_all(rows.reshape(holders, capacity, -1), BOTH, split_axis=0, c...  8.78 us
    all_to_all x1, starting transfers between devices, on_device(): got_ids = lax.all_to_all(ids, BOTH, split_axis=0, concat_axis=0, tiled=True)  8.11 us
    pallas_call x1, Pallas kernels, state_of(): pl.pallas_call(state_kernel, out_shape=[jax.ShapeDtypeStruct((blocks, STA...  4.42 us
    ppermute x3, starting transfers between devices, on_device(): lax.ppermute(pair, 'tm', [(i, i - k) for i in range(k, size)])  3.88 us
  transfers between devices with their start and end apart: 7, of which 4 were waited for; matrix products, arithmetic and copies ran while one was open for 0% of the time, Pallas kernels for 14%

profile of v3, /device:TPU:0, one launch (start us, length us, event | category | flops | bytes accessed | tf_op | source)
XLA Modules:
  0.0 155.3 jit_solution(11109833039017696212)
XLA Ops:
  0.6 4.4 %state.1 = (f32[8,64,512]{2,1,0:T(8,128)}, f32[8,1,512]{2,1,0:T(1,128)}, f32[64,256]{1,0:T(8,128)}, f32[72,512]{1,0:T(8,128)}) custom-call(bf16[2048,512]{1,0:T(8,128)(2,1)} %bitcast.12, bf16[2048,128]{1,0:T(8,128)(2,1)} %bitcast.18, f32[8,2048]{1,0:T(8,128)} %bitcast.23), custom_call_target="tpu_custom_call" | custom-call | flops 268435456 | bytes 4194304 | tf_op jit(solution)/shard_map/state/pallas_call | solution.py:103
  5.0 3.0 %collective-permute-start = (f32[72,512]{1,0:T(8,128)}, f32[72,512]{1,0:T(8,128)S(1)}, u32[]{:S(2)}, u32[]{:S(2)}) collective-permute-start(f32[72,512]{1,0:T(8,128)} %get-tuple-element.20), channel_id=1, source_target_pairs={{0,4},{4,0},{8,12},{12,8},{16,20},{20,16},{24,28},{28,24},{1,5},{5... | collective-permute-start | bytes 442376 | tf_op jit(solution)/shard_map/ppermute | solution.py:426
  8.0 3.1 %slots.1 = (s32[1,2048]{1,0:T(1,128)}, s32[1,32]{1,0:T(1,128)}, s32[32,1,128]{2,1,0:T(1,128)}) custom-call(s32[1,2048]{1,0:T(1,128)} %bitcast.27, s32[1,2048]{1,0:T(1,128)} %row_ref.1), custom_call_target="tpu_custom_call" | custom-call | flops 67108864 | bytes 16384 | tf_op jit(solution)/shard_map/slots/pallas_call | solution.py:256
  11.1 1.0 collective-permute-done.end_ref
  12.1 1.0 broadcast_select_fusion.1
  13.1 0.0 copy-start.1
  13.2 1.3 collective-permute-start.1
  14.4 1.3 collective-permute-start.2
  15.8 1.3 collective-permute-start.3
  17.1 8.1 %all-to-all-start = ((s32[32,1,128]{2,1,0:T(1,128)}), s32[32,1,128]{2,1,0:T(1,128)S(1)}, u32[]{:S(2)}, u32[]{:S(2)}) async-start(s32[32,1,128]{2,1,0:T(1,128)} %get-tuple-element.17), calls=%async_computation | async-start | bytes 32768 | tf_op jit(solution)/shard_map/all_to_all | solution.py:421
  25.2 0.0 copy-done.1
  25.2 6.1 %local.2 = (f32[2048,256]{1,0:T(8,128)}, f32[2048,256]{1,0:T(8,128)}) custom-call(bf16[2048,512]{1,0:T(8,128)(2,1)} %bitcast.13, bf16[2048,128]{1,0:T(8,128)(2,1)} %bitcast.19, f32[64,256]{1,0:T(8,128)} %get-tuple-element.22.cumul_ref, f32[1,8]{1,0:T(1,128)} %bitcast.28, f32[8,64,512]{2,1,0:T(8,128)} %get-tuple-element.23.carried_ref, ...), custom_call_target="tpu_custom_call" | custom-call | flops 301989888 | bytes 5242880 | tf_op jit(solution)/shard_map/local/pallas_call | solution.py:180
  31.3 0.0 copy-done.2
  31.3 1.4 all-to-all-done.refs_3_
  32.7 0.0 collective-permute-done.1.refs_0_
  32.7 0.0 collective-permute-done.2.refs_1_
  32.7 0.0 copy-start.5
  32.7 0.0 collective-permute-done.3.refs_2_
  32.7 0.6 copy-done.3
  33.3 0.1 copy-done.4
  33.3 0.1 copy-done.5
  33.4 0.0 copy-done.6
  33.4 7.4 %send.2._ = bf16[4096,256]{1,0:T(8,128)(2,1)} custom-call(s32[1]{0:T(128)} %bitcast.2.sides_ref, s32[1,32]{1,0:T(1,128)} %get-tuple-element.18.starts_ref, s32[1,2048]{1,0:T(1,128)} %get-tuple-element.21.place_ref, bf16[2048,128]{1,0:T(8,128)(2,1)} %bitcast.20, f32[2048,256]{1,0:T(8,128)} %get-tuple-element.26.local_ref, ...), custom_call_target="tpu_custom_call" | custom-call | flops 2650800128 | bytes 6291456 | tf_op jit(solution)/shard_map/send/pallas_call | solution.py:332
  40.9 4.7 %all-to-all-start.2 = ((bf16[32,128,256]{2,1,0:T(8,128)(2,1)}), bf16[32,128,256]{2,1,0:T(8,128)(2,1)S(1)}, u32[]{:S(2)}, u32[]{:S(2)}) async-start(bf16[32,128,256]{2,1,0:T(8,128)(2,1)} %bitcast.16), calls=%async_computation.2 | async-start | bytes 4194304 | tf_op jit(solution)/shard_map/all_to_all | solution.py:439
  45.6 6.1 %local.3 = (f32[2048,256]{1,0:T(8,128)}, f32[2048,256]{1,0:T(8,128)}) custom-call(bf16[2048,512]{1,0:T(8,128)(2,1)} %bitcast.14, bf16[2048,128]{1,0:T(8,128)(2,1)} %bitcast.21, f32[64,256]{1,0:T(8,128)} %get-tuple-element.22.cumul_ref, f32[1,8]{1,0:T(1,128)} %bitcast.29, f32[8,64,512]{2,1,0:T(8,128)} %get-tuple-element.23.carried_ref, ...), custom_call_target="tpu_custom_call" | custom-call | flops 301989888 | bytes 5242880 | tf_op jit(solution)/shard_map/local/pallas_call | solution.py:180
  51.7 7.4 %send.3 = bf16[4096,256]{1,0:T(8,128)(2,1)} custom-call(s32[1]{0:T(128)} %bitcast.2.sides_ref, s32[1,32]{1,0:T(1,128)} %get-tuple-element.18.starts_ref, s32[1,2048]{1,0:T(1,128)} %get-tuple-element.21.place_ref, bf16[2048,128]{1,0:T(8,128)(2,1)} %bitcast.22, f32[2048,256]{1,0:T(8,128)} %get-tuple-element.28.local_ref, ...), custom_call_target="tpu_custom_call" | custom-call | flops 2650800128 | bytes 6291456 | tf_op jit(solution)/shard_map/send/pallas_call | solution.py:332
  59.1 35.2 %all-to-all-done.2 = bf16[32,128,256]{2,1,0:T(8,128)(2,1)S(1)} async-done(((bf16[32,128,256]{2,1,0:T(8,128)(2,1)}), bf16[32,128,256]{2,1,0:T(8,128)(2,1)S(1)}, u32[]{:S(2)}, u32[]{:S(2)}) %all-to-all-start.2) | async-done | bytes 2097184 | tf_op jit(solution)/shard_map/all_to_all | solution.py:439
  94.3 1.3 copy-done
  95.7 4.1 %all-to-all-start.1 = ((bf16[32,128,256]{2,1,0:T(8,128)(2,1)}), bf16[32,128,256]{2,1,0:T(8,128)(2,1)}, u32[]{:S(2)}, u32[]{:S(2)}) async-start(bf16[32,128,256]{2,1,0:T(8,128)(2,1)} %bitcast.17), calls=%async_computation.1 | async-start | bytes 4194304 | tf_op jit(solution)/shard_map/all_to_all | solution.py:439
  99.8 6.8 %update.2 = (bf16[1536,512]{1,0:T(8,128)(2,1)}, f32[1536,512]{1,0:T(8,128)}) custom-call(s32[32,128]{1,0:T(8,128)} %bitcast.24, bf16[4096,256]{1,0:T(8,128)(2,1)} %bitcast.15, bf16[1536,512]{1,0:T(8,128)(2,1)} %table_ref.3, f32[1536,512]{1,0:T(8,128)} %accum_ref.3), custom_call_target="tpu_custom_call" | custom-call | flops 3221225472 | bytes 4718592 | tf_op jit(solution)/shard_map/update/pallas_call | solution.py:381
  106.6 42.1 %all-to-all-done.1 = bf16[32,128,256]{2,1,0:T(8,128)(2,1)} async-done(((bf16[32,128,256]{2,1,0:T(8,128)(2,1)}), bf16[32,128,256]{2,1,0:T(8,128)(2,1)}, u32[]{:S(2)}, u32[]{:S(2)}) %all-to-all-start.1) | async-done | bytes 2097184 | tf_op jit(solution)/shard_map/all_to_all | solution.py:439
  148.7 6.7 %update.3 = (bf16[1536,512]{1,0:T(8,128)(2,1)}, f32[1536,512]{1,0:T(8,128)}) custom-call(s32[32,128]{1,0:T(8,128)} %bitcast.25, bf16[4096,256]{1,0:T(8,128)(2,1)} %bitcast.9.got_ref, bf16[1536,512]{1,0:T(8,128)(2,1)} %table_ref.3, f32[1536,512]{1,0:T(8,128)} %accum_ref.3, ...), custom_call_target="tpu_custom_call", output_to_operand_aliasing={{0}: (4, {}), {1}: (5, {})} | custom-call | flops 3221225472 | bytes 4718592 | tf_op jit(solution)/shard_map/update/pallas_call | solution.py:381
  (9 shorter events, 0.1 us)
Async XLA Ops:
  5.0 7.0 %collective-permute-start = (f32[72,512]{1,0:T(8,128)}, f32[72,512]{1,0:T(8,128)S(1)}, u32[]{:S(2)}, u32[]{:S(2)}) collective-permute-start(f32[72,512]{1,0:T(8,128)} %get-tuple-element.20), channel_id=1, source_target_pairs={{0,4},{4,0},{8,12},{12,8},{16,20},{20,16},{24,28},{28,24},{1,5},{5... | collective-permute-start | bytes 442376 | tf_op jit(solution)/shard_map/ppermute | solution.py:426
  12.1 19.2 %copy-start.2 = (f32[72,512]{1,0:T(8,128)}, f32[72,512]{1,0:T(8,128)S(1)}, u32[]{:S(2)}) copy-start(f32[72,512]{1,0:T(8,128)S(1)} %collective-permute-done.end_ref) | copy-start | bytes 442372
  13.1 12.0 %copy-start.1 = (f32[72,512]{1,0:T(8,128)}, f32[72,512]{1,0:T(8,128)S(1)}, u32[]{:S(2)}) copy-start(f32[72,512]{1,0:T(8,128)S(1)} %pad_maximum_fusion._) | copy-start | bytes 442372
  13.2 19.5 %collective-permute-start.1 = (f32[72,512]{1,0:T(8,128)S(1)}, f32[72,512]{1,0:T(8,128)S(1)}, u32[]{:S(2)}, u32[]{:S(2)}) collective-permute-start(f32[72,512]{1,0:T(8,128)S(1)} %pad_maximum_fusion._), channel_id=1, source_target_pairs={{8,0},{12,4},{16,8},{20,12},{24,16},{28,20},{9,1},{13,5},{17,9},{2... | collective-permute-start | bytes 442376 | tf_op jit(solution)/shard_map/ppermute | solution.py:430
  14.4 18.2 %collective-permute-start.2 = (f32[72,512]{1,0:T(8,128)S(1)}, f32[72,512]{1,0:T(8,128)S(1)}, u32[]{:S(2)}, u32[]{:S(2)}) collective-permute-start(f32[72,512]{1,0:T(8,128)S(1)} %pad_maximum_fusion._), channel_id=1, source_target_pairs={{16,0},{20,4},{24,8},{28,12},{17,1},{21,5},{25,9},{29,13},{18,2},{... | collective-permute-start | bytes 442376 | tf_op jit(solution)/shard_map/ppermute | solution.py:430
  15.8 16.9 %collective-permute-start.3 = (f32[72,512]{1,0:T(8,128)S(1)}, f32[72,512]{1,0:T(8,128)S(1)}, u32[]{:S(2)}, u32[]{:S(2)}) collective-permute-start(f32[72,512]{1,0:T(8,128)S(1)} %pad_maximum_fusion._), channel_id=1, source_target_pairs={{24,0},{28,4},{25,1},{29,5},{26,2},{30,6},{27,3},{31,7}} | collective-permute-start | bytes 442376 | tf_op jit(solution)/shard_map/ppermute | solution.py:430
  17.1 15.6 %all-to-all-start = ((s32[32,1,128]{2,1,0:T(1,128)}), s32[32,1,128]{2,1,0:T(1,128)S(1)}, u32[]{:S(2)}, u32[]{:S(2)}) async-start(s32[32,1,128]{2,1,0:T(1,128)} %get-tuple-element.17), calls=%async_computation | async-start | bytes 32768 | tf_op jit(solution)/shard_map/all_to_all | solution.py:421
  32.7 0.6 copy-start.3
  32.7 0.7 copy-start.4
  32.7 0.7 copy-start.5
  32.7 0.7 copy-start.6
  40.9 53.5 %all-to-all-start.2 = ((bf16[32,128,256]{2,1,0:T(8,128)(2,1)}), bf16[32,128,256]{2,1,0:T(8,128)(2,1)S(1)}, u32[]{:S(2)}, u32[]{:S(2)}) async-start(bf16[32,128,256]{2,1,0:T(8,128)(2,1)} %bitcast.16), calls=%async_computation.2 | async-start | bytes 4194304 | tf_op jit(solution)/shard_map/all_to_all | solution.py:439
  94.3 1.3 copy-start
  95.7 53.0 %all-to-all-start.1 = ((bf16[32,128,256]{2,1,0:T(8,128)(2,1)}), bf16[32,128,256]{2,1,0:T(8,128)(2,1)}, u32[]{:S(2)}, u32[]{:S(2)}) async-start(bf16[32,128,256]{2,1,0:T(8,128)(2,1)} %bitcast.17), calls=%async_computation.1 | async-start | bytes 4194304 | tf_op jit(solution)/shard_map/all_to_all | solution.py:439

commit v4 on v3

--- a/solution.py
+++ b/solution.py
@@ -14,7 +14,7 @@
 PARTS = 2
 PART_HEADS = HEADS // PARTS
 BOTH = ("tm", "table")
-VMEM_BYTES = 60 * 1024 * 1024
+MIB = 1024 * 1024
 
 learn_rate = 1.0
 
@@ -22,8 +22,8 @@
 bf16 = jnp.bfloat16
 
 
-def params():
-    return pltpu.CompilerParams(vmem_limit_bytes=VMEM_BYTES)
+def params(mib=60):
+    return pltpu.CompilerParams(vmem_limit_bytes=mib * MIB)
 
 
 def cost(flops, moved, exps=0):
@@ -389,7 +389,7 @@
             jax.ShapeDtypeStruct(accum.shape, f32),
         ],
         input_output_aliases={4 + k: k for k in range(len(before))},
-        compiler_params=params(),
+        compiler_params=params(60 if part else 40),
         cost_estimate=cost(2 * owned * got.shape[0] * width, 12 * owned * width),
         name="update",
     )(ids, got, table, accum, *before)

time: 156 us -> 155 us (level)
  local copies, waits for them, and re-layouts: 2.1 us -> 4.06 us
  Pallas kernels: 48 us -> 46.1 us
    unnamed x14 -> x18, local copies, waits for them, and re-layouts: 2.09 us -> 4.05 us
    pallas_call x2, Pallas kernels: 13.5 us -> 11.5 us  [updated(): pl.pallas_call(functools.partial(update_kernel, tile), grid=(owned // til...]
  transfers between devices with their start and end apart: 7 -> 7, of which waited for: 4 -> 4; matrix products, arithmetic and copies ran while one was open for 0% -> 0% of each run, Pallas kernels for 14% -> 13%
where the time goes in v4:
time: 155 us; the launch traced here: 154 us
  waiting for transfers between devices  78.2 us (50%)
  Pallas kernels  46.1 us (30%)
  starting transfers between devices  23.7 us (15%)
  local copies, waits for them, and re-layouts  4.06 us (3%)
    all_to_all x2, waiting for transfers between devices, on_device(): lax.all_to_all(rows.reshape(holders, capacity, -1), BOTH, split_axis=0, c...  75.9 us
    pallas_call x2, Pallas kernels, sent_rows(): pl.pallas_call(functools.partial(send_kernel, blocks, tiles), grid=(block...  14.9 us
    pallas_call x2, Pallas kernels, local_rows(): pl.pallas_call(functools.partial(local_kernel, part), grid=(blocks // ste...  12.2 us
    pallas_call x2, Pallas kernels, updated(): pl.pallas_call(functools.partial(update_kernel, tile), grid=(owned // til...  11.5 us
    all_to_all x2, starting transfers between devices, on_device(): lax.all_to_all(rows.reshape(holders, capacity, -1), BOTH, split_axis=0, c...  8.79 us
    all_to_all x1, starting transfers between devices, on_device(): got_ids = lax.all_to_all(ids, BOTH, split_axis=0, concat_axis=0, tiled=True)  8.11 us
    pallas_call x1, Pallas kernels, state_of(): pl.pallas_call(state_kernel, out_shape=[jax.ShapeDtypeStruct((blocks, STA...  4.42 us
    unnamed x18, local copies, waits for them, and re-layouts  4.05 us
  transfers between devices with their start and end apart: 7, of which 4 were waited for; matrix products, arithmetic and copies ran while one was open for 0% of the time, Pallas kernels for 13%

profile of v4, /device:TPU:0, one launch (start us, length us, event | category | flops | bytes accessed | tf_op | source)
XLA Modules:
  0.0 154.0 jit_solution(12006216088503870275)
XLA Ops:
  0.6 4.4 %state.1 = (f32[8,64,512]{2,1,0:T(8,128)}, f32[8,1,512]{2,1,0:T(1,128)}, f32[64,256]{1,0:T(8,128)}, f32[72,512]{1,0:T(8,128)}) custom-call(bf16[2048,512]{1,0:T(8,128)(2,1)} %bitcast.15, bf16[2048,128]{1,0:T(8,128)(2,1)} %bitcast.20, f32[8,2048]{1,0:T(8,128)} %bitcast.25), custom_call_target="tpu_custom_call" | custom-call | flops 268435456 | bytes 4194304 | tf_op jit(solution)/shard_map/state/pallas_call | solution.py:103
  5.0 3.0 %collective-permute-start = (f32[72,512]{1,0:T(8,128)}, f32[72,512]{1,0:T(8,128)S(1)}, u32[]{:S(2)}, u32[]{:S(2)}) collective-permute-start(f32[72,512]{1,0:T(8,128)} %get-tuple-element.20), channel_id=1, source_target_pairs={{0,4},{4,0},{8,12},{12,8},{16,20},{20,16},{24,28},{28,24},{1,5},{5... | collective-permute-start | bytes 442376 | tf_op jit(solution)/shard_map/ppermute | solution.py:426
  8.0 3.1 %slots.1 = (s32[1,2048]{1,0:T(1,128)}, s32[1,32]{1,0:T(1,128)}, s32[32,1,128]{2,1,0:T(1,128)}) custom-call(s32[1,2048]{1,0:T(1,128)} %bitcast.27, s32[1,2048]{1,0:T(1,128)} %row_ref.1), custom_call_target="tpu_custom_call" | custom-call | flops 67108864 | bytes 16384 | tf_op jit(solution)/shard_map/slots/pallas_call | solution.py:256
  11.1 1.0 collective-permute-done.end_ref
  12.1 1.0 broadcast_select_fusion.1
  13.1 0.0 copy-start.4
  13.2 1.3 collective-permute-start.1
  14.4 1.3 collective-permute-start.2
  15.8 1.3 collective-permute-start.3
  17.1 8.1 %all-to-all-start = ((s32[32,1,128]{2,1,0:T(1,128)}), s32[32,1,128]{2,1,0:T(1,128)S(1)}, u32[]{:S(2)}, u32[]{:S(2)}) async-start(s32[32,1,128]{2,1,0:T(1,128)} %get-tuple-element.17), calls=%async_computation | async-start | bytes 32768 | tf_op jit(solution)/shard_map/all_to_all | solution.py:421
  25.2 6.1 %local.2 = (f32[2048,256]{1,0:T(8,128)}, f32[2048,256]{1,0:T(8,128)}) custom-call(bf16[2048,512]{1,0:T(8,128)(2,1)} %bitcast.16, bf16[2048,128]{1,0:T(8,128)(2,1)} %bitcast.21, f32[64,256]{1,0:T(8,128)} %get-tuple-element.22.cumul_ref, f32[1,8]{1,0:T(1,128)} %bitcast.28, f32[8,64,512]{2,1,0:T(8,128)} %get-tuple-element.23.carried_ref, ...), custom_call_target="tpu_custom_call" | custom-call | flops 301989888 | bytes 5242880 | tf_op jit(solution)/shard_map/local/pallas_call | solution.py:180
  31.3 1.4 all-to-all-done.refs_3_
  32.7 0.0 collective-permute-done.1.refs_0_
  32.7 0.0 collective-permute-done.2.refs_1_
  32.7 0.0 collective-permute-done.3.refs_2_
  32.7 0.6 copy-done
  33.3 0.1 copy-done.6
  33.3 0.1 copy-done.7
  33.4 0.0 copy-done.8
  33.4 7.4 %send.2._ = bf16[4096,256]{1,0:T(8,128)(2,1)} custom-call(s32[1]{0:T(128)} %bitcast.2.sides_ref, s32[1,32]{1,0:T(1,128)} %get-tuple-element.18.starts_ref, s32[1,2048]{1,0:T(1,128)} %get-tuple-element.21.place_ref, bf16[2048,128]{1,0:T(8,128)(2,1)} %bitcast.22, f32[2048,256]{1,0:T(8,128)} %get-tuple-element.26.local_ref, ...), custom_call_target="tpu_custom_call" | custom-call | flops 2650800128 | bytes 6291456 | tf_op jit(solution)/shard_map/send/pallas_call | solution.py:332
  40.9 4.7 %all-to-all-start.2 = ((bf16[32,128,256]{2,1,0:T(8,128)(2,1)}), bf16[32,128,256]{2,1,0:T(8,128)(2,1)S(1)}, u32[]{:S(2)}, u32[]{:S(2)}) async-start(bf16[32,128,256]{2,1,0:T(8,128)(2,1)} %bitcast.18), calls=%async_computation.2 | async-start | bytes 4194304 | tf_op jit(solution)/shard_map/all_to_all | solution.py:439
  45.6 6.1 %local.3 = (f32[2048,256]{1,0:T(8,128)}, f32[2048,256]{1,0:T(8,128)}) custom-call(bf16[2048,512]{1,0:T(8,128)(2,1)} %bitcast.17, bf16[2048,128]{1,0:T(8,128)(2,1)} %bitcast.23, f32[64,256]{1,0:T(8,128)} %get-tuple-element.22.cumul_ref, f32[1,8]{1,0:T(1,128)} %bitcast.29, f32[8,64,512]{2,1,0:T(8,128)} %get-tuple-element.23.carried_ref, ...), custom_call_target="tpu_custom_call" | custom-call | flops 301989888 | bytes 5242880 | tf_op jit(solution)/shard_map/local/pallas_call | solution.py:180
  51.7 7.5 %send.3 = bf16[4096,256]{1,0:T(8,128)(2,1)} custom-call(s32[1]{0:T(128)} %bitcast.2.sides_ref, s32[1,32]{1,0:T(1,128)} %get-tuple-element.18.starts_ref, s32[1,2048]{1,0:T(1,128)} %get-tuple-element.21.place_ref, bf16[2048,128]{1,0:T(8,128)(2,1)} %bitcast.24, f32[2048,256]{1,0:T(8,128)} %get-tuple-element.28.local_ref, ...), custom_call_target="tpu_custom_call" | custom-call | flops 2650800128 | bytes 6291456 | tf_op jit(solution)/shard_map/send/pallas_call | solution.py:332
  59.2 35.2 %all-to-all-done.2 = bf16[32,128,256]{2,1,0:T(8,128)(2,1)S(1)} async-done(((bf16[32,128,256]{2,1,0:T(8,128)(2,1)}), bf16[32,128,256]{2,1,0:T(8,128)(2,1)S(1)}, u32[]{:S(2)}, u32[]{:S(2)}) %all-to-all-start.2) | async-done | bytes 2097184 | tf_op jit(solution)/shard_map/all_to_all | solution.py:439
  94.4 4.1 %all-to-all-start.1 = ((bf16[32,128,256]{2,1,0:T(8,128)(2,1)}), bf16[32,128,256]{2,1,0:T(8,128)(2,1)}, u32[]{:S(2)}, u32[]{:S(2)}) async-start(bf16[32,128,256]{2,1,0:T(8,128)(2,1)} %bitcast.19), calls=%async_computation.1 | async-start | bytes 4194304 | tf_op jit(solution)/shard_map/all_to_all | solution.py:439
  98.5 0.0 copy-done.1
  98.5 0.0 copy-start.2
  98.5 1.9 %copy-done.2 = f32[1536,512]{1,0:T(8,128)S(1)} copy-done((f32[1536,512]{1,0:T(8,128)S(1)}, f32[1536,512]{1,0:T(8,128)}, u32[]{:S(2)}) %copy-start.2) | copy-done | bytes 3145752
  100.4 1.4 copy-done.3
  101.8 4.9 %update.2 = (bf16[1536,512]{1,0:T(8,128)(2,1)}, f32[1536,512]{1,0:T(8,128)}) custom-call(s32[32,128]{1,0:T(8,128)S(1)} %bitcast.14, bf16[4096,256]{1,0:T(8,128)(2,1)S(1)} %bitcast.12, bf16[1536,512]{1,0:T(8,128)(2,1)S(1)} %copy-done.3, f32[1536,512]{1,0:T(8,128)S(1)} %copy-done.2), custom_call_target="tpu_custom_call" | custom-call | flops 3221225472 | bytes 4718592 | tf_op jit(solution)/shard_map/update/pallas_call | solution.py:381
  106.6 40.7 %all-to-all-done.1 = bf16[32,128,256]{2,1,0:T(8,128)(2,1)} async-done(((bf16[32,128,256]{2,1,0:T(8,128)(2,1)}), bf16[32,128,256]{2,1,0:T(8,128)(2,1)}, u32[]{:S(2)}, u32[]{:S(2)}) %all-to-all-start.1) | async-done | bytes 2097184 | tf_op jit(solution)/shard_map/all_to_all | solution.py:439
  147.3 6.7 %update.3 = (bf16[1536,512]{1,0:T(8,128)(2,1)}, f32[1536,512]{1,0:T(8,128)}) custom-call(s32[32,128]{1,0:T(8,128)} %bitcast.13, bf16[4096,256]{1,0:T(8,128)(2,1)} %bitcast.9.got_ref, bf16[1536,512]{1,0:T(8,128)(2,1)} %table_ref.3, f32[1536,512]{1,0:T(8,128)} %accum_ref.3, ...), custom_call_target="tpu_custom_call", output_to_operand_aliasing={{0}: (4, {}), {1}: (5, {})} | custom-call | flops 3221225472 | bytes 4718592 | tf_op jit(solution)/shard_map/update/pallas_call | solution.py:381
  (13 shorter events, 0.1 us)
Async XLA Ops:
  5.0 7.0 %collective-permute-start = (f32[72,512]{1,0:T(8,128)}, f32[72,512]{1,0:T(8,128)S(1)}, u32[]{:S(2)}, u32[]{:S(2)}) collective-permute-start(f32[72,512]{1,0:T(8,128)} %get-tuple-element.20), channel_id=1, source_target_pairs={{0,4},{4,0},{8,12},{12,8},{16,20},{20,16},{24,28},{28,24},{1,5},{5... | collective-permute-start | bytes 442376 | tf_op jit(solution)/shard_map/ppermute | solution.py:426
  12.1 19.2 %copy-start.5 = (f32[72,512]{1,0:T(8,128)}, f32[72,512]{1,0:T(8,128)S(1)}, u32[]{:S(2)}) copy-start(f32[72,512]{1,0:T(8,128)S(1)} %collective-permute-done.end_ref) | copy-start | bytes 442372
  13.1 12.0 %copy-start.4 = (f32[72,512]{1,0:T(8,128)}, f32[72,512]{1,0:T(8,128)S(1)}, u32[]{:S(2)}) copy-start(f32[72,512]{1,0:T(8,128)S(1)} %pad_maximum_fusion._) | copy-start | bytes 442372
  13.2 19.5 %collective-permute-start.1 = (f32[72,512]{1,0:T(8,128)S(1)}, f32[72,512]{1,0:T(8,128)S(1)}, u32[]{:S(2)}, u32[]{:S(2)}) collective-permute-start(f32[72,512]{1,0:T(8,128)S(1)} %pad_maximum_fusion._), channel_id=1, source_target_pairs={{8,0},{12,4},{16,8},{20,12},{24,16},{28,20},{9,1},{13,5},{17,9},{2... | collective-permute-start | bytes 442376 | tf_op jit(solution)/shard_map/ppermute | solution.py:430
  14.4 18.2 %collective-permute-start.2 = (f32[72,512]{1,0:T(8,128)S(1)}, f32[72,512]{1,0:T(8,128)S(1)}, u32[]{:S(2)}, u32[]{:S(2)}) collective-permute-start(f32[72,512]{1,0:T(8,128)S(1)} %pad_maximum_fusion._), channel_id=1, source_target_pairs={{16,0},{20,4},{24,8},{28,12},{17,1},{21,5},{25,9},{29,13},{18,2},{... | collective-permute-start | bytes 442376 | tf_op jit(solution)/shard_map/ppermute | solution.py:430
  15.8 16.9 %collective-permute-start.3 = (f32[72,512]{1,0:T(8,128)S(1)}, f32[72,512]{1,0:T(8,128)S(1)}, u32[]{:S(2)}, u32[]{:S(2)}) collective-permute-start(f32[72,512]{1,0:T(8,128)S(1)} %pad_maximum_fusion._), channel_id=1, source_target_pairs={{24,0},{28,4},{25,1},{29,5},{26,2},{30,6},{27,3},{31,7}} | collective-permute-start | bytes 442376 | tf_op jit(solution)/shard_map/ppermute | solution.py:430
  17.1 15.6 %all-to-all-start = ((s32[32,1,128]{2,1,0:T(1,128)}), s32[32,1,128]{2,1,0:T(1,128)S(1)}, u32[]{:S(2)}, u32[]{:S(2)}) async-start(s32[32,1,128]{2,1,0:T(1,128)} %get-tuple-element.17), calls=%async_computation | async-start | bytes 32768 | tf_op jit(solution)/shard_map/all_to_all | solution.py:421
  32.7 0.6 copy-start
  32.7 0.7 copy-start.6
  32.7 0.7 copy-start.7
  32.7 0.8 copy-start.8
  40.9 53.5 %all-to-all-start.2 = ((bf16[32,128,256]{2,1,0:T(8,128)(2,1)}), bf16[32,128,256]{2,1,0:T(8,128)(2,1)S(1)}, u32[]{:S(2)}, u32[]{:S(2)}) async-start(bf16[32,128,256]{2,1,0:T(8,128)(2,1)} %bitcast.18), calls=%async_computation.2 | async-start | bytes 4194304 | tf_op jit(solution)/shard_map/all_to_all | solution.py:439
  94.4 4.1 %copy-start.1 = (s32[32,1,128]{2,1,0:T(1,128)S(1)}, s32[32,1,128]{2,1,0:T(1,128)}, u32[]{:S(2)}) copy-start(s32[32,1,128]{2,1,0:T(1,128)} %copy-done) | copy-start | bytes 49156
  94.4 53.0 %all-to-all-start.1 = ((bf16[32,128,256]{2,1,0:T(8,128)(2,1)}), bf16[32,128,256]{2,1,0:T(8,128)(2,1)}, u32[]{:S(2)}, u32[]{:S(2)}) async-start(bf16[32,128,256]{2,1,0:T(8,128)(2,1)} %bitcast.19), calls=%async_computation.1 | async-start | bytes 4194304 | tf_op jit(solution)/shard_map/all_to_all | solution.py:439
  98.5 1.9 %copy-start.2 = (f32[1536,512]{1,0:T(8,128)S(1)}, f32[1536,512]{1,0:T(8,128)}, u32[]{:S(2)}) copy-start(f32[1536,512]{1,0:T(8,128)} %accum_ref.3) | copy-start | bytes 9437188
  100.4 1.4 copy-start.3

commit v5 on v4

--- a/solution.py
+++ b/solution.py
@@ -269,7 +269,7 @@
 def send_kernel(
     blocks, tiles, sides_ref, starts_ref, place_ref, bc_ref, local_ref, fade_ref, end_ref, *refs,
 ):
-    hops, (_, out_ref, high, low, rows, ordered, done) = refs[:-7], refs[-7:]
+    hops, (out_ref, high, low, rows, ordered, done) = refs[:-6], refs[-6:]
     step = pl.program_id(0)
     events, width = rows.shape
     block = events // blocks
@@ -320,7 +320,7 @@
             copy(k).wait()
 
 
-def sent_rows(part, sides, starts, place, bc, local, fade, partner, hops, capacity, earlier):
+def sent_rows(part, sides, starts, place, bc, local, fade, partner, hops, capacity):
     events, width = local.shape
     holders = starts.shape[1]
     blocks, tiles = 2, 1
@@ -340,8 +340,7 @@
             pl.BlockSpec((block, width), at),
             pl.BlockSpec((block, width), at),
         ]
-        + [pl.BlockSpec((hop.shape[0], width), lambda i: (0, part)) for hop in (partner, *hops)]
-        + [pl.BlockSpec(memory_space=pl.ANY)],
+        + [pl.BlockSpec((hop.shape[0], width), lambda i: (0, part)) for hop in (partner, *hops)],
         out_specs=pl.BlockSpec(memory_space=pltpu.HBM),
         out_shape=jax.ShapeDtypeStruct((holders * capacity, width), bf16),
         scratch_shapes=[
@@ -354,7 +353,7 @@
         compiler_params=params(),
         cost_estimate=cost(2 * ordered * events * width, 12 * events * width),
         name="send",
-    )(sides, starts, place, bc, local, fade, partner, *hops, earlier)
+    )(sides, starts, place, bc, local, fade, partner, *hops)
 
 
 def update_kernel(tile, ids_ref, got_ref, table_ref, accum_ref, *refs):
@@ -395,9 +394,7 @@
     )(ids, got, table, accum, *before)
 
 
-def pair_state(side, end, partner):
-    early = jnp.where(side == 0, end, partner)
-    late = jnp.where(side == 0, partner, end)
+def joined(early, late):
     return jnp.concatenate(
         [
             early[:STATE] + jnp.exp(early[STATE : STATE + 1]) * late[:STATE],
@@ -419,27 +416,36 @@
 
     place, starts, ids = slots(owner.reshape(1, events), item_row, holders, capacity)
     got_ids = lax.all_to_all(ids, BOTH, split_axis=0, concat_axis=0, tiled=True)
-    ids = got_ids.reshape(-1, 128)
     skip = skip_gain.reshape(1, HEADS)
 
     carried, after, cumul, end = state_of(grad, bc, decay)
     partner = lax.ppermute(end, "tm", [(i, i ^ 1) for i in range(size)])
     place, partner = lax.optimization_barrier((place, partner))
-    pair = pair_state(side, end, partner)
-    hops = [
-        lax.ppermute(pair, "tm", [(i, i - k) for i in range(k, size)]) for k in range(2, size, 2)
-    ]
-
-    new, earlier = (), pair
+    pair = joined(jnp.where(side == 0, end, partner), jnp.where(side == 0, partner, end))
+    of_part = lambda part, earlier: local_rows(
+        part, grad, bc, cumul, skip, carried, after, earlier
+    )
+    first = of_part(0, pair)
+    hops, reach, k = [], pair, 2
+    while k < size:
+        hop = lax.ppermute(reach, "tm", [(i, i - k) for i in range(k, size)])
+        if k == 2:
+            hop, first = lax.optimization_barrier((hop, first))
+        hops.append(hop)
+        reach, k = joined(reach, hop), 2 * k
+
+    new, earlier = (), None
     for part in range(PARTS):
-        local, fade = local_rows(part, grad, bc, cumul, skip, carried, after, earlier)
+        local, fade = of_part(part, earlier) if part else first
         rows = sent_rows(
-            part, sides, starts, place, bc, local, fade, partner, hops, capacity, got_ids
+            part, sides, starts, place, bc, local, fade, partner, hops, capacity
         )
+        if part == 0:
+            rows, got_ids = lax.optimization_barrier((rows, got_ids))
         got = lax.all_to_all(
             rows.reshape(holders, capacity, -1), BOTH, split_axis=0, concat_axis=0, tiled=True
         )
-        new = updated(part, ids, got.reshape(holders * capacity, -1), table, accum, new)
+        new = updated(part, got_ids.reshape(-1, 128), got.reshape(holders * capacity, -1), table, accum, new)
         earlier = rows
     return new
 

time: 155 us -> 153 us (0.987)
  starting transfers between devices: 23.7 us -> 22 us
    ppermute x3 -> x2, waiting for transfers between devices: 0.01 us -> 1.8 us  [on_device(): hop = lax.ppermute(reach, 'tm', [(i, i - k) for i in range(k, size)])]
    ppermute x3 -> x2, starting transfers between devices: 3.88 us -> 2.58 us  [on_device(): hop = lax.ppermute(reach, 'tm', [(i, i - k) for i in range(k, size)])]
    unnamed x18 -> x14, local copies, waits for them, and re-layouts: 4.05 us -> 3.97 us
  transfers between devices with their start and end apart: 7 -> 6, of which waited for: 4 -> 4; matrix products, arithmetic and copies ran while one was open for 0% -> 0% of each run, Pallas kernels for 13% -> 13%
where the time goes in v5:
time: 153 us
  waiting for transfers between devices  78.7 us (51%)
  Pallas kernels  46.1 us (30%)
  starting transfers between devices  22 us (14%)
  local copies, waits for them, and re-layouts  3.99 us (3%)
    all_to_all x2, waiting for transfers between devices, on_device(): lax.all_to_all(rows.reshape(holders, capacity, -1), BOTH, split_axis=0, c...  75.9 us
    pallas_call x2, Pallas kernels, sent_rows(): pl.pallas_call(functools.partial(send_kernel, blocks, tiles), grid=(block...  14.9 us
    pallas_call x2, Pallas kernels, local_rows(): pl.pallas_call(functools.partial(local_kernel, part), grid=(blocks // ste...  12.2 us
    pallas_call x2, Pallas kernels, updated(): pl.pallas_call(functools.partial(update_kernel, tile), grid=(owned // til...  11.5 us
    all_to_all x2, starting transfers between devices, on_device(): lax.all_to_all(rows.reshape(holders, capacity, -1), BOTH, split_axis=0, c...  8.33 us
    all_to_all x1, starting transfers between devices, on_device(): got_ids = lax.all_to_all(ids, BOTH, split_axis=0, concat_axis=0, tiled=True)  8.11 us
    pallas_call x1, Pallas kernels, state_of(): pl.pallas_call(state_kernel, out_shape=[jax.ShapeDtypeStruct((blocks, STA...  4.42 us
    unnamed x14, local copies, waits for them, and re-layouts  3.97 us
  transfers between devices with their start and end apart: 6, of which 4 were waited for; matrix products, arithmetic and copies ran while one was open for 0% of the time, Pallas kernels for 13%

profile of v5, /device:TPU:0, one launch (start us, length us, event | category | flops | bytes accessed | tf_op | source)
XLA Modules:
  0.0 152.7 jit_solution(17757588237176151795)
XLA Ops:
  0.6 4.4 %state.1 = (f32[8,64,512]{2,1,0:T(8,128)}, f32[8,1,512]{2,1,0:T(1,128)}, f32[64,256]{1,0:T(8,128)}, f32[72,512]{1,0:T(8,128)}) custom-call(bf16[2048,512]{1,0:T(8,128)(2,1)} %bitcast.16, bf16[2048,128]{1,0:T(8,128)(2,1)} %bitcast.21, f32[8,2048]{1,0:T(8,128)} %bitcast.26), custom_call_target="tpu_custom_call" | custom-call | flops 268435456 | bytes 4194304 | tf_op jit(solution)/shard_map/state/pallas_call | solution.py:103
  5.0 3.0 %collective-permute-start = (f32[72,512]{1,0:T(8,128)}, f32[72,512]{1,0:T(8,128)S(1)}, u32[]{:S(2)}, u32[]{:S(2)}) collective-permute-start(f32[72,512]{1,0:T(8,128)} %get-tuple-element.24), channel_id=1, source_target_pairs={{0,4},{4,0},{8,12},{12,8},{16,20},{20,16},{24,28},{28,24},{1,5},{5... | collective-permute-start | bytes 442376 | tf_op jit(solution)/shard_map/ppermute | solution.py:422
  8.0 3.1 %slots.1 = (s32[1,2048]{1,0:T(1,128)}, s32[1,32]{1,0:T(1,128)}, s32[32,1,128]{2,1,0:T(1,128)}) custom-call(s32[1,2048]{1,0:T(1,128)} %bitcast.29, s32[1,2048]{1,0:T(1,128)} %row_ref.1), custom_call_target="tpu_custom_call" | custom-call | flops 67108864 | bytes 16384 | tf_op jit(solution)/shard_map/slots/pallas_call | solution.py:256
  11.1 1.0 collective-permute-done.end_ref
  12.1 1.0 broadcast_select_fusion.1
  13.1 0.0 copy-start.4
  13.2 1.3 collective-permute-start.1
  14.4 0.0 copy-done.4
  14.5 6.1 %local.2 = (f32[2048,256]{1,0:T(8,128)}, f32[2048,256]{1,0:T(8,128)}) custom-call(bf16[2048,512]{1,0:T(8,128)(2,1)} %bitcast.17, bf16[2048,128]{1,0:T(8,128)(2,1)} %bitcast.22, f32[64,256]{1,0:T(8,128)} %get-tuple-element.27.cumul_ref, f32[1,8]{1,0:T(1,128)} %bitcast.30, f32[8,64,512]{2,1,0:T(8,128)} %get-tuple-element.28.carried_ref, ...), custom_call_target="tpu_custom_call" | custom-call | flops 301989888 | bytes 5242880 | tf_op jit(solution)/shard_map/local/pallas_call | solution.py:180
  20.6 0.0 copy-done.5
  20.6 0.0 collective-permute-done.1.refs_0_
  20.6 0.0 copy-start.3
  20.7 1.3 collective-permute-start.2
  22.0 8.1 %all-to-all-start = ((s32[32,1,128]{2,1,0:T(1,128)}), s32[32,1,128]{2,1,0:T(1,128)S(1)}, u32[]{:S(2)}, u32[]{:S(2)}) async-start(s32[32,1,128]{2,1,0:T(1,128)} %get-tuple-element.35), calls=%async_computation | async-start | bytes 32768 | tf_op jit(solution)/shard_map/all_to_all | solution.py:418
  30.1 1.8 %collective-permute-done.2.refs_1_ = f32[72,512]{1,0:T(8,128)S(1)} collective-permute-done((f32[72,512]{1,0:T(8,128)S(1)}, f32[72,512]{1,0:T(8,128)S(1)}, u32[]{:S(2)}, u32[]{:S(2)}) %collective-permute-start.2) | collective-permute-done | bytes 147488 | tf_op jit(solution)/shard_map/ppermute | solution.py:431
  31.9 0.0 copy-done.3
  31.9 0.7 copy-done.6
  32.6 7.4 %send.2._ = bf16[4096,256]{1,0:T(8,128)(2,1)} custom-call(s32[1]{0:T(128)} %bitcast.sides_ref, s32[1,32]{1,0:T(1,128)} %get-tuple-element.22.starts_ref, s32[1,2048]{1,0:T(1,128)} %get-tuple-element.25.place_ref, bf16[2048,128]{1,0:T(8,128)(2,1)} %bitcast.23, f32[2048,256]{1,0:T(8,128)} %get-tuple-element.32.local_ref, ...), custom_call_target="tpu_custom_call" | custom-call | flops 2650800128 | bytes 6291456 | tf_op jit(solution)/shard_map/send/pallas_call | solution.py:332
  40.0 0.0 all-to-all-done
  40.0 0.0 copy-start
  40.0 4.2 %all-to-all-start.2 = ((bf16[32,128,256]{2,1,0:T(8,128)(2,1)}), bf16[32,128,256]{2,1,0:T(8,128)(2,1)S(1)}, u32[]{:S(2)}, u32[]{:S(2)}) async-start(bf16[32,128,256]{2,1,0:T(8,128)(2,1)} %bitcast.19), calls=%async_computation.2 | async-start | bytes 4194304 | tf_op jit(solution)/shard_map/all_to_all | solution.py:445
  44.3 6.1 %local.3 = (f32[2048,256]{1,0:T(8,128)}, f32[2048,256]{1,0:T(8,128)}) custom-call(bf16[2048,512]{1,0:T(8,128)(2,1)} %bitcast.18, bf16[2048,128]{1,0:T(8,128)(2,1)} %bitcast.24, f32[64,256]{1,0:T(8,128)} %get-tuple-element.27.cumul_ref, f32[1,8]{1,0:T(1,128)} %bitcast.31, f32[8,64,512]{2,1,0:T(8,128)} %get-tuple-element.28.carried_ref, ...), custom_call_target="tpu_custom_call" | custom-call | flops 301989888 | bytes 5242880 | tf_op jit(solution)/shard_map/local/pallas_call | solution.py:180
  50.3 7.5 %send.3 = bf16[4096,256]{1,0:T(8,128)(2,1)} custom-call(s32[1]{0:T(128)} %bitcast.sides_ref, s32[1,32]{1,0:T(1,128)} %get-tuple-element.22.starts_ref, s32[1,2048]{1,0:T(1,128)} %get-tuple-element.25.place_ref, bf16[2048,128]{1,0:T(8,128)(2,1)} %bitcast.25, f32[2048,256]{1,0:T(8,128)} %get-tuple-element.38.local_ref, ...), custom_call_target="tpu_custom_call" | custom-call | flops 2650800128 | bytes 6291456 | tf_op jit(solution)/shard_map/send/pallas_call | solution.py:332
  57.8 35.2 %all-to-all-done.2 = bf16[32,128,256]{2,1,0:T(8,128)(2,1)S(1)} async-done(((bf16[32,128,256]{2,1,0:T(8,128)(2,1)}), bf16[32,128,256]{2,1,0:T(8,128)(2,1)S(1)}, u32[]{:S(2)}, u32[]{:S(2)}) %all-to-all-start.2) | async-done | bytes 2097184 | tf_op jit(solution)/shard_map/all_to_all | solution.py:445
  93.0 4.1 %all-to-all-start.1 = ((bf16[32,128,256]{2,1,0:T(8,128)(2,1)}), bf16[32,128,256]{2,1,0:T(8,128)(2,1)}, u32[]{:S(2)}, u32[]{:S(2)}) async-start(bf16[32,128,256]{2,1,0:T(8,128)(2,1)} %bitcast.20), calls=%async_computation.1 | async-start | bytes 4194304 | tf_op jit(solution)/shard_map/all_to_all | solution.py:445
  97.1 0.0 copy-done
  97.1 0.0 copy-start.1
  97.1 1.9 %copy-done.1 = f32[1536,512]{1,0:T(8,128)S(1)} copy-done((f32[1536,512]{1,0:T(8,128)S(1)}, f32[1536,512]{1,0:T(8,128)}, u32[]{:S(2)}) %copy-start.1) | copy-done | bytes 3145752
  99.0 1.4 copy-done.2
  100.4 4.9 %update.2 = (bf16[1536,512]{1,0:T(8,128)(2,1)}, f32[1536,512]{1,0:T(8,128)}) custom-call(s32[32,128]{1,0:T(8,128)S(1)} %bitcast.14, bf16[4096,256]{1,0:T(8,128)(2,1)S(1)} %bitcast.13, bf16[1536,512]{1,0:T(8,128)(2,1)S(1)} %copy-done.2, f32[1536,512]{1,0:T(8,128)S(1)} %copy-done.1), custom_call_target="tpu_custom_call" | custom-call | flops 3221225472 | bytes 4718592 | tf_op jit(solution)/shard_map/update/pallas_call | solution.py:380
  105.3 40.7 %all-to-all-done.1 = bf16[32,128,256]{2,1,0:T(8,128)(2,1)} async-done(((bf16[32,128,256]{2,1,0:T(8,128)(2,1)}), bf16[32,128,256]{2,1,0:T(8,128)(2,1)}, u32[]{:S(2)}, u32[]{:S(2)}) %all-to-all-start.1) | async-done | bytes 2097184 | tf_op jit(solution)/shard_map/all_to_all | solution.py:445
  146.0 6.7 %update.3 = (bf16[1536,512]{1,0:T(8,128)(2,1)}, f32[1536,512]{1,0:T(8,128)}) custom-call(s32[32,128]{1,0:T(8,128)} %bitcast.15, bf16[4096,256]{1,0:T(8,128)(2,1)} %bitcast.10.got_ref, bf16[1536,512]{1,0:T(8,128)(2,1)} %table_ref.3, f32[1536,512]{1,0:T(8,128)} %accum_ref.3, ...), custom_call_target="tpu_custom_call", output_to_operand_aliasing={{0}: (4, {}), {1}: (5, {})} | custom-call | flops 3221225472 | bytes 4718592 | tf_op jit(solution)/shard_map/update/pallas_call | solution.py:380
  (11 shorter events, 0.1 us)
Async XLA Ops:
  5.0 7.0 %collective-permute-start = (f32[72,512]{1,0:T(8,128)}, f32[72,512]{1,0:T(8,128)S(1)}, u32[]{:S(2)}, u32[]{:S(2)}) collective-permute-start(f32[72,512]{1,0:T(8,128)} %get-tuple-element.24), channel_id=1, source_target_pairs={{0,4},{4,0},{8,12},{12,8},{16,20},{20,16},{24,28},{28,24},{1,5},{5... | collective-permute-start | bytes 442376 | tf_op jit(solution)/shard_map/ppermute | solution.py:422
  12.1 8.5 %copy-start.5 = (f32[72,512]{1,0:T(8,128)}, f32[72,512]{1,0:T(8,128)S(1)}, u32[]{:S(2)}) copy-start(f32[72,512]{1,0:T(8,128)S(1)} %collective-permute-done.end_ref) | copy-start | bytes 442372
  13.1 1.3 copy-start.4
  13.2 7.4 %collective-permute-start.1 = (f32[72,512]{1,0:T(8,128)S(1)}, f32[72,512]{1,0:T(8,128)S(1)}, u32[]{:S(2)}, u32[]{:S(2)}) collective-permute-start(f32[72,512]{1,0:T(8,128)S(1)} %pad_maximum_fusion._), channel_id=1, source_target_pairs={{8,0},{12,4},{16,8},{20,12},{24,16},{28,20},{9,1},{13,5},{17,9},{2... | collective-permute-start | bytes 442376 | tf_op jit(solution)/shard_map/ppermute | solution.py:431
  20.6 11.3 %copy-start.3 = (f32[72,512]{1,0:T(8,128)}, f32[72,512]{1,0:T(8,128)S(1)}, u32[]{:S(2)}) copy-start(f32[72,512]{1,0:T(8,128)S(1)} %collective-permute-done.1.refs_0_) | copy-start | bytes 442372
  20.7 11.2 %collective-permute-start.2 = (f32[72,512]{1,0:T(8,128)S(1)}, f32[72,512]{1,0:T(8,128)S(1)}, u32[]{:S(2)}, u32[]{:S(2)}) collective-permute-start(f32[72,512]{1,0:T(8,128)S(1)} %pad_maximum_fusion.1), channel_id=1, source_target_pairs={{16,0},{20,4},{24,8},{28,12},{17,1},{21,5},{25,9},{29,13},{18,2},{... | collective-permute-start | bytes 442376 | tf_op jit(solution)/shard_map/ppermute | solution.py:431
  22.0 18.0 %all-to-all-start = ((s32[32,1,128]{2,1,0:T(1,128)}), s32[32,1,128]{2,1,0:T(1,128)S(1)}, u32[]{:S(2)}, u32[]{:S(2)}) async-start(s32[32,1,128]{2,1,0:T(1,128)} %get-tuple-element.35), calls=%async_computation | async-start | bytes 32768 | tf_op jit(solution)/shard_map/all_to_all | solution.py:418
  31.9 0.7 copy-start.6
  40.0 57.1 %copy-start = (s32[32,1,128]{2,1,0:T(1,128)}, s32[32,1,128]{2,1,0:T(1,128)S(1)}, u32[]{:S(2)}) copy-start(s32[32,1,128]{2,1,0:T(1,128)S(1)} %all-to-all-done) | copy-start | bytes 49156
  40.0 53.0 %all-to-all-start.2 = ((bf16[32,128,256]{2,1,0:T(8,128)(2,1)}), bf16[32,128,256]{2,1,0:T(8,128)(2,1)S(1)}, u32[]{:S(2)}, u32[]{:S(2)}) async-start(bf16[32,128,256]{2,1,0:T(8,128)(2,1)} %bitcast.19), calls=%async_computation.2 | async-start | bytes 4194304 | tf_op jit(solution)/shard_map/all_to_all | solution.py:445
  93.0 53.0 %all-to-all-start.1 = ((bf16[32,128,256]{2,1,0:T(8,128)(2,1)}), bf16[32,128,256]{2,1,0:T(8,128)(2,1)}, u32[]{:S(2)}, u32[]{:S(2)}) async-start(bf16[32,128,256]{2,1,0:T(8,128)(2,1)} %bitcast.20), calls=%async_computation.1 | async-start | bytes 4194304 | tf_op jit(solution)/shard_map/all_to_all | solution.py:445
  97.1 1.9 %copy-start.1 = (f32[1536,512]{1,0:T(8,128)S(1)}, f32[1536,512]{1,0:T(8,128)}, u32[]{:S(2)}) copy-start(f32[1536,512]{1,0:T(8,128)} %accum_ref.3) | copy-start | bytes 9437188
  99.0 1.4 copy-start.2

commit v6 on v5

--- a/solution.py
+++ b/solution.py
@@ -350,7 +350,7 @@
             pltpu.VMEM((ordered + capacity, width), bf16),
             pltpu.SemaphoreType.DMA((holders,)),
         ],
-        compiler_params=params(),
+        compiler_params=params(58),
         cost_estimate=cost(2 * ordered * events * width, 12 * events * width),
         name="send",
     )(sides, starts, place, bc, local, fade, partner, *hops)

time: 153 us -> 153 us (level)
  no operation moved by 1% of the time
where the time goes in v6:
time: 153 us
  waiting for transfers between devices  78.7 us (51%)
  Pallas kernels  46.1 us (30%)
  starting transfers between devices  22 us (14%)
  local copies, waits for them, and re-layouts  3.99 us (3%)
    all_to_all x2, waiting for transfers between devices, on_device(): lax.all_to_all(rows.reshape(holders, capacity, -1), BOTH, split_axis=0, c...  75.9 us
    pallas_call x2, Pallas kernels, sent_rows(): pl.pallas_call(functools.partial(send_kernel, blocks, tiles), grid=(block...  14.9 us
    pallas_call x2, Pallas kernels, local_rows(): pl.pallas_call(functools.partial(local_kernel, part), grid=(blocks // ste...  12.2 us
    pallas_call x2, Pallas kernels, updated(): pl.pallas_call(functools.partial(update_kernel, tile), grid=(owned // til...  11.5 us
    all_to_all x2, starting transfers between devices, on_device(): lax.all_to_all(rows.reshape(holders, capacity, -1), BOTH, split_axis=0, c...  8.33 us
    all_to_all x1, starting transfers between devices, on_device(): got_ids = lax.all_to_all(ids, BOTH, split_axis=0, concat_axis=0, tiled=True)  8.11 us
    pallas_call x1, Pallas kernels, state_of(): pl.pallas_call(state_kernel, out_shape=[jax.ShapeDtypeStruct((blocks, STA...  4.42 us
    unnamed x14, local copies, waits for them, and re-layouts  3.97 us
  transfers between devices with their start and end apart: 6, of which 4 were waited for; matrix products, arithmetic and copies ran while one was open for 0% of the time, Pallas kernels for 13%

profile of v6, /device:TPU:0, one launch (start us, length us, event | category | flops | bytes accessed | tf_op | source)
XLA Modules:
  0.0 152.7 jit_solution(17757588237176151795)
XLA Ops:
  0.6 4.4 %state.1 = (f32[8,64,512]{2,1,0:T(8,128)}, f32[8,1,512]{2,1,0:T(1,128)}, f32[64,256]{1,0:T(8,128)}, f32[72,512]{1,0:T(8,128)}) custom-call(bf16[2048,512]{1,0:T(8,128)(2,1)} %bitcast.16, bf16[2048,128]{1,0:T(8,128)(2,1)} %bitcast.21, f32[8,2048]{1,0:T(8,128)} %bitcast.26), custom_call_target="tpu_custom_call" | custom-call | flops 268435456 | bytes 4194304 | tf_op jit(solution)/shard_map/state/pallas_call | solution.py:103
  5.0 3.0 %collective-permute-start = (f32[72,512]{1,0:T(8,128)}, f32[72,512]{1,0:T(8,128)S(1)}, u32[]{:S(2)}, u32[]{:S(2)}) collective-permute-start(f32[72,512]{1,0:T(8,128)} %get-tuple-element.24), channel_id=1, source_target_pairs={{0,4},{4,0},{8,12},{12,8},{16,20},{20,16},{24,28},{28,24},{1,5},{5... | collective-permute-start | bytes 442376 | tf_op jit(solution)/shard_map/ppermute | solution.py:422
  8.0 3.1 %slots.1 = (s32[1,2048]{1,0:T(1,128)}, s32[1,32]{1,0:T(1,128)}, s32[32,1,128]{2,1,0:T(1,128)}) custom-call(s32[1,2048]{1,0:T(1,128)} %bitcast.29, s32[1,2048]{1,0:T(1,128)} %row_ref.1), custom_call_target="tpu_custom_call" | custom-call | flops 67108864 | bytes 16384 | tf_op jit(solution)/shard_map/slots/pallas_call | solution.py:256
  11.1 1.0 collective-permute-done.end_ref
  12.1 1.0 broadcast_select_fusion.1
  13.1 0.0 copy-start.4
  13.2 1.3 collective-permute-start.1
  14.4 0.0 copy-done.4
  14.5 6.1 %local.2 = (f32[2048,256]{1,0:T(8,128)}, f32[2048,256]{1,0:T(8,128)}) custom-call(bf16[2048,512]{1,0:T(8,128)(2,1)} %bitcast.17, bf16[2048,128]{1,0:T(8,128)(2,1)} %bitcast.22, f32[64,256]{1,0:T(8,128)} %get-tuple-element.27.cumul_ref, f32[1,8]{1,0:T(1,128)} %bitcast.30, f32[8,64,512]{2,1,0:T(8,128)} %get-tuple-element.28.carried_ref, ...), custom_call_target="tpu_custom_call" | custom-call | flops 301989888 | bytes 5242880 | tf_op jit(solution)/shard_map/local/pallas_call | solution.py:180
  20.6 0.0 copy-done.5
  20.6 0.0 collective-permute-done.1.refs_0_
  20.6 0.0 copy-start.3
  20.7 1.3 collective-permute-start.2
  22.0 8.1 %all-to-all-start = ((s32[32,1,128]{2,1,0:T(1,128)}), s32[32,1,128]{2,1,0:T(1,128)S(1)}, u32[]{:S(2)}, u32[]{:S(2)}) async-start(s32[32,1,128]{2,1,0:T(1,128)} %get-tuple-element.35), calls=%async_computation | async-start | bytes 32768 | tf_op jit(solution)/shard_map/all_to_all | solution.py:418
  30.1 1.8 %collective-permute-done.2.refs_1_ = f32[72,512]{1,0:T(8,128)S(1)} collective-permute-done((f32[72,512]{1,0:T(8,128)S(1)}, f32[72,512]{1,0:T(8,128)S(1)}, u32[]{:S(2)}, u32[]{:S(2)}) %collective-permute-start.2) | collective-permute-done | bytes 147488 | tf_op jit(solution)/shard_map/ppermute | solution.py:431
  31.9 0.0 copy-done.3
  31.9 0.7 copy-done.6
  32.6 7.4 %send.2._ = bf16[4096,256]{1,0:T(8,128)(2,1)} custom-call(s32[1]{0:T(128)} %bitcast.sides_ref, s32[1,32]{1,0:T(1,128)} %get-tuple-element.22.starts_ref, s32[1,2048]{1,0:T(1,128)} %get-tuple-element.25.place_ref, bf16[2048,128]{1,0:T(8,128)(2,1)} %bitcast.23, f32[2048,256]{1,0:T(8,128)} %get-tuple-element.32.local_ref, ...), custom_call_target="tpu_custom_call" | custom-call | flops 2650800128 | bytes 6291456 | tf_op jit(solution)/shard_map/send/pallas_call | solution.py:332
  40.0 0.0 all-to-all-done
  40.0 0.0 copy-start
  40.0 4.2 %all-to-all-start.2 = ((bf16[32,128,256]{2,1,0:T(8,128)(2,1)}), bf16[32,128,256]{2,1,0:T(8,128)(2,1)S(1)}, u32[]{:S(2)}, u32[]{:S(2)}) async-start(bf16[32,128,256]{2,1,0:T(8,128)(2,1)} %bitcast.19), calls=%async_computation.2 | async-start | bytes 4194304 | tf_op jit(solution)/shard_map/all_to_all | solution.py:445
  44.3 6.1 %local.3 = (f32[2048,256]{1,0:T(8,128)}, f32[2048,256]{1,0:T(8,128)}) custom-call(bf16[2048,512]{1,0:T(8,128)(2,1)} %bitcast.18, bf16[2048,128]{1,0:T(8,128)(2,1)} %bitcast.24, f32[64,256]{1,0:T(8,128)} %get-tuple-element.27.cumul_ref, f32[1,8]{1,0:T(1,128)} %bitcast.31, f32[8,64,512]{2,1,0:T(8,128)} %get-tuple-element.28.carried_ref, ...), custom_call_target="tpu_custom_call" | custom-call | flops 301989888 | bytes 5242880 | tf_op jit(solution)/shard_map/local/pallas_call | solution.py:180
  50.3 7.5 %send.3 = bf16[4096,256]{1,0:T(8,128)(2,1)} custom-call(s32[1]{0:T(128)} %bitcast.sides_ref, s32[1,32]{1,0:T(1,128)} %get-tuple-element.22.starts_ref, s32[1,2048]{1,0:T(1,128)} %get-tuple-element.25.place_ref, bf16[2048,128]{1,0:T(8,128)(2,1)} %bitcast.25, f32[2048,256]{1,0:T(8,128)} %get-tuple-element.38.local_ref, ...), custom_call_target="tpu_custom_call" | custom-call | flops 2650800128 | bytes 6291456 | tf_op jit(solution)/shard_map/send/pallas_call | solution.py:332
  57.8 35.2 %all-to-all-done.2 = bf16[32,128,256]{2,1,0:T(8,128)(2,1)S(1)} async-done(((bf16[32,128,256]{2,1,0:T(8,128)(2,1)}), bf16[32,128,256]{2,1,0:T(8,128)(2,1)S(1)}, u32[]{:S(2)}, u32[]{:S(2)}) %all-to-all-start.2) | async-done | bytes 2097184 | tf_op jit(solution)/shard_map/all_to_all | solution.py:445
  93.0 4.1 %all-to-all-start.1 = ((bf16[32,128,256]{2,1,0:T(8,128)(2,1)}), bf16[32,128,256]{2,1,0:T(8,128)(2,1)}, u32[]{:S(2)}, u32[]{:S(2)}) async-start(bf16[32,128,256]{2,1,0:T(8,128)(2,1)} %bitcast.20), calls=%async_computation.1 | async-start | bytes 4194304 | tf_op jit(solution)/shard_map/all_to_all | solution.py:445
  97.1 0.0 copy-done
  97.1 0.0 copy-start.1
  97.1 1.9 %copy-done.1 = f32[1536,512]{1,0:T(8,128)S(1)} copy-done((f32[1536,512]{1,0:T(8,128)S(1)}, f32[1536,512]{1,0:T(8,128)}, u32[]{:S(2)}) %copy-start.1) | copy-done | bytes 3145752
  99.0 1.4 copy-done.2
  100.4 4.9 %update.2 = (bf16[1536,512]{1,0:T(8,128)(2,1)}, f32[1536,512]{1,0:T(8,128)}) custom-call(s32[32,128]{1,0:T(8,128)S(1)} %bitcast.14, bf16[4096,256]{1,0:T(8,128)(2,1)S(1)} %bitcast.13, bf16[1536,512]{1,0:T(8,128)(2,1)S(1)} %copy-done.2, f32[1536,512]{1,0:T(8,128)S(1)} %copy-done.1), custom_call_target="tpu_custom_call" | custom-call | flops 3221225472 | bytes 4718592 | tf_op jit(solution)/shard_map/update/pallas_call | solution.py:380
  105.3 40.7 %all-to-all-done.1 = bf16[32,128,256]{2,1,0:T(8,128)(2,1)} async-done(((bf16[32,128,256]{2,1,0:T(8,128)(2,1)}), bf16[32,128,256]{2,1,0:T(8,128)(2,1)}, u32[]{:S(2)}, u32[]{:S(2)}) %all-to-all-start.1) | async-done | bytes 2097184 | tf_op jit(solution)/shard_map/all_to_all | solution.py:445
  146.0 6.7 %update.3 = (bf16[1536,512]{1,0:T(8,128)(2,1)}, f32[1536,512]{1,0:T(8,128)}) custom-call(s32[32,128]{1,0:T(8,128)} %bitcast.15, bf16[4096,256]{1,0:T(8,128)(2,1)} %bitcast.10.got_ref, bf16[1536,512]{1,0:T(8,128)(2,1)} %table_ref.3, f32[1536,512]{1,0:T(8,128)} %accum_ref.3, ...), custom_call_target="tpu_custom_call", output_to_operand_aliasing={{0}: (4, {}), {1}: (5, {})} | custom-call | flops 3221225472 | bytes 4718592 | tf_op jit(solution)/shard_map/update/pallas_call | solution.py:380
  (11 shorter events, 0.1 us)
Async XLA Ops:
  5.0 7.0 %collective-permute-start = (f32[72,512]{1,0:T(8,128)}, f32[72,512]{1,0:T(8,128)S(1)}, u32[]{:S(2)}, u32[]{:S(2)}) collective-permute-start(f32[72,512]{1,0:T(8,128)} %get-tuple-element.24), channel_id=1, source_target_pairs={{0,4},{4,0},{8,12},{12,8},{16,20},{20,16},{24,28},{28,24},{1,5},{5... | collective-permute-start | bytes 442376 | tf_op jit(solution)/shard_map/ppermute | solution.py:422
  12.1 8.5 %copy-start.5 = (f32[72,512]{1,0:T(8,128)}, f32[72,512]{1,0:T(8,128)S(1)}, u32[]{:S(2)}) copy-start(f32[72,512]{1,0:T(8,128)S(1)} %collective-permute-done.end_ref) | copy-start | bytes 442372
  13.1 1.3 copy-start.4
  13.2 7.4 %collective-permute-start.1 = (f32[72,512]{1,0:T(8,128)S(1)}, f32[72,512]{1,0:T(8,128)S(1)}, u32[]{:S(2)}, u32[]{:S(2)}) collective-permute-start(f32[72,512]{1,0:T(8,128)S(1)} %pad_maximum_fusion._), channel_id=1, source_target_pairs={{8,0},{12,4},{16,8},{20,12},{24,16},{28,20},{9,1},{13,5},{17,9},{2... | collective-permute-start | bytes 442376 | tf_op jit(solution)/shard_map/ppermute | solution.py:431
  20.6 11.3 %copy-start.3 = (f32[72,512]{1,0:T(8,128)}, f32[72,512]{1,0:T(8,128)S(1)}, u32[]{:S(2)}) copy-start(f32[72,512]{1,0:T(8,128)S(1)} %collective-permute-done.1.refs_0_) | copy-start | bytes 442372
  20.7 11.2 %collective-permute-start.2 = (f32[72,512]{1,0:T(8,128)S(1)}, f32[72,512]{1,0:T(8,128)S(1)}, u32[]{:S(2)}, u32[]{:S(2)}) collective-permute-start(f32[72,512]{1,0:T(8,128)S(1)} %pad_maximum_fusion.1), channel_id=1, source_target_pairs={{16,0},{20,4},{24,8},{28,12},{17,1},{21,5},{25,9},{29,13},{18,2},{... | collective-permute-start | bytes 442376 | tf_op jit(solution)/shard_map/ppermute | solution.py:431
  22.0 18.0 %all-to-all-start = ((s32[32,1,128]{2,1,0:T(1,128)}), s32[32,1,128]{2,1,0:T(1,128)S(1)}, u32[]{:S(2)}, u32[]{:S(2)}) async-start(s32[32,1,128]{2,1,0:T(1,128)} %get-tuple-element.35), calls=%async_computation | async-start | bytes 32768 | tf_op jit(solution)/shard_map/all_to_all | solution.py:418
  31.9 0.7 copy-start.6
  40.0 57.1 %copy-start = (s32[32,1,128]{2,1,0:T(1,128)}, s32[32,1,128]{2,1,0:T(1,128)S(1)}, u32[]{:S(2)}) copy-start(s32[32,1,128]{2,1,0:T(1,128)S(1)} %all-to-all-done) | copy-start | bytes 49156
  40.0 53.0 %all-to-all-start.2 = ((bf16[32,128,256]{2,1,0:T(8,128)(2,1)}), bf16[32,128,256]{2,1,0:T(8,128)(2,1)S(1)}, u32[]{:S(2)}, u32[]{:S(2)}) async-start(bf16[32,128,256]{2,1,0:T(8,128)(2,1)} %bitcast.19), calls=%async_computation.2 | async-start | bytes 4194304 | tf_op jit(solution)/shard_map/all_to_all | solution.py:445
  93.0 53.0 %all-to-all-start.1 = ((bf16[32,128,256]{2,1,0:T(8,128)(2,1)}), bf16[32,128,256]{2,1,0:T(8,128)(2,1)}, u32[]{:S(2)}, u32[]{:S(2)}) async-start(bf16[32,128,256]{2,1,0:T(8,128)(2,1)} %bitcast.20), calls=%async_computation.1 | async-start | bytes 4194304 | tf_op jit(solution)/shard_map/all_to_all | solution.py:445
  97.1 1.9 %copy-start.1 = (f32[1536,512]{1,0:T(8,128)S(1)}, f32[1536,512]{1,0:T(8,128)}, u32[]{:S(2)}) copy-start(f32[1536,512]{1,0:T(8,128)} %accum_ref.3) | copy-start | bytes 9437188
  99.0 1.4 copy-start.2
